TPU v7x, 32 devices: a whole 2x2x4 slice. The times are simulated.
32 devices in a mesh: tok: 8 (over z, x), feat: 4 (over y, core).
Axes of the slice: x: 2, y: 2, z: 4, core: 2. Of those that a mesh axis runs over, the one named last changes fastest.
Arguments:
- tokens: float32 [768, 4096], P('feat', 'tok'), may hold values from -6 to 6
- timesteps: int32 [16], P('tok'), may hold values from 0 to 999
- labels: int32 [16], P('tok'), may hold values from 0 to 1000
- class_table: bfloat16 [768, 1001], P('feat'), may hold values from -6 to 6
- ada_weight: bfloat16 [6, 768, 768], P(None, 'tok', 'feat'), may hold values from -0.21875 to 0.21875
- ada_bias: float32 [6, 768], P(None, 'feat'), may hold values from -3 to 3
- qkv_weight: bfloat16 [3, 768, 768], P(None, 'tok', 'feat'), may hold values from -0.21875 to 0.21875
- qv_bias: float32 [2, 768], P(None, 'feat'), may hold values from -2 to 2
- proj_weight: bfloat16 [768, 768], P('tok', 'feat'), may hold values from -0.875 to 0.875
- proj_bias: float32 [768], P('feat'), may hold values from -2 to 2
- fc1_weight: bfloat16 [768, 3072], P('tok', 'feat'), may hold values from -0.21875 to 0.21875
- fc1_bias: float32 [3072], P('feat'), may hold values from -2 to 2
- fc2_weight: bfloat16 [768, 3072], P('tok', 'feat'), may hold values from -0.109375 to 0.109375
- fc2_bias: float32 [768], P('feat'), may hold values from -2 to 2
- cotangent: float32 [768, 4096], P('feat', 'tok'), may hold values from -6 to 6
Outputs:
- output: float32 [768, 4096], P('feat', 'tok')
- tokens_grad: float32 [768, 4096], P('feat', 'tok')
- class_grad: float32 [768, 1001], P('feat')
- ada_weight_grad: float32 [6, 768, 768], P(None, 'tok', 'feat')
- ada_bias_grad: float32 [6, 768], P(None, 'feat')
- qkv_weight_grad: float32 [3, 768, 768], P(None, 'tok', 'feat')
- qv_bias_grad: float32 [2, 768], P(None, 'feat')
- proj_weight_grad: float32 [768, 768], P('tok', 'feat')
- proj_bias_grad: float32 [768], P('feat')
- fc1_weight_grad: float32 [768, 3072], P('tok', 'feat')
- fc1_bias_grad: float32 [3072], P('feat')
- fc2_weight_grad: float32 [768, 3072], P('tok', 'feat')
- fc2_bias_grad: float32 [768], P('feat')
All inputs are finite; a program needn't handle non-finite values.
Results may differ from a plain program's by a relative error of at most 0.02.
The roundings to bfloat16 on the way count: a program that leaves them out, or rounds other values in their place, can miss the bound.
Values may be sent and summed in bfloat16 or wider, within the bound.
A program may use at most 128 MiB of HBM per device.

v0:
```python
from functools import partial
import math

import jax
import jax.numpy as jnp
from jax import lax
from jax.sharding import PartitionSpec as P

D = 768
HEAD_DIM = 64


def time_features(step_ids, feat_count):
    half_width = feat_count // 2
    frequency = jnp.exp(-math.log(10000.0) * jnp.arange(half_width, dtype=jnp.float32) / half_width)
    angles = step_ids.astype(jnp.float32)[:, None] * frequency[None, :]
    return jnp.concatenate([jnp.cos(angles), jnp.sin(angles)], axis=-1)


def normalize(values_in):
    mean_val = lax.psum(jnp.sum(values_in, -1), "feat") / D
    centered = values_in - mean_val[..., None]
    variance = lax.psum(jnp.sum(centered * centered, -1), "feat") / D
    inverse = lax.rsqrt(variance + 1e-06)
    return ((values_in - mean_val[..., None]) * inverse[..., None], inverse)


def norm_back(grad_norm, normed, inverse):
    first_sum, second_sum = lax.psum(
        (jnp.sum(grad_norm, -1), jnp.sum(grad_norm * normed, -1)), "feat"
    )
    return inverse[..., None] * (
        grad_norm - first_sum[..., None] / D - normed * second_sum[..., None] / D
    )


def gather_features(values_in):
    return lax.all_gather(values_in, "feat", axis=1, tiled=True)


def gather_grads(values_in):
    return lax.all_gather(values_in, "feat", axis=1, tiled=True)


def reduce_features(term):
    return lax.psum_scatter(term, "feat", scatter_dimension=1, tiled=True)


def reduce_grads(term):
    return lax.psum_scatter(
        term.astype(jnp.bfloat16), "feat", scatter_dimension=1, tiled=True
    ).astype(jnp.float32)


def per_device(
    tokens,
    timesteps,
    labels,
    class_table,
    ada_weight,
    ada_bias,
    qkv_weight,
    qv_bias,
    proj_weight,
    proj_bias,
    fc1_weight,
    fc1_bias,
    fc2_weight,
    fc2_bias,
    cotangent,
):
    f32 = jnp.float32
    bf16 = jnp.bfloat16
    feat_width, row_count = tokens.shape
    latent_count = timesteps.shape[0]
    seq_len = row_count // latent_count
    head_count = feat_width // HEAD_DIM
    score_scale = HEAD_DIM ** (-0.5)
    offset = lax.axis_index("feat") * feat_width
    lat_shape = (latent_count, seq_len, feat_width)
    head_shape = (latent_count, seq_len, head_count, HEAD_DIM)
    waves = lax.dynamic_slice_in_dim(time_features(timesteps, D), offset, feat_width, 1)
    condition = jnp.take(class_table, labels, axis=1).T.astype(f32) + waves
    cond_low = jax.nn.silu(condition).astype(bf16)
    cond_full = lax.all_gather(cond_low, "feat", axis=1, tiled=True)
    ada_full, qkv_full, proj_full, fc1_full, fc2_full = (
        lax.all_gather(ada_weight, "tok", axis=1, tiled=True),
        lax.all_gather(qkv_weight, "tok", axis=1, tiled=True),
        lax.all_gather(proj_weight, "tok", axis=0, tiled=True),
        lax.all_gather(fc1_weight, "tok", axis=0, tiled=True),
        lax.all_gather(fc2_weight, "tok", axis=0, tiled=True),
    )
    modulation = (
        jnp.einsum("lk,jkc->ljc", cond_full, ada_full, preferred_element_type=f32) + ada_bias[None]
    )
    shift_one = modulation[:, 0, None, :]
    scale_one = modulation[:, 1, None, :]
    gate_one = modulation[:, 2, None, :]
    shift_two = modulation[:, 3, None, :]
    scale_two = modulation[:, 4, None, :]
    gate_two = modulation[:, 5, None, :]
    field_in = tokens.T.reshape(lat_shape)
    normed_one, inverse_one = normalize(field_in)
    hidden_one = (
        (normed_one * (1.0 + scale_one) + shift_one).astype(bf16).reshape(row_count, feat_width)
    )
    full_one = gather_features(hidden_one)
    projected = jnp.einsum("rk,jkc->jrc", full_one, qkv_full, preferred_element_type=f32)
    queries = (projected[0] + qv_bias[0]).astype(bf16).reshape(head_shape)
    keys_low = projected[1].astype(bf16).reshape(head_shape)
    values_low = (projected[2] + qv_bias[1]).astype(bf16).reshape(head_shape)
    scores = (
        jnp.einsum("lqhd,lkhd->lhqk", queries, keys_low, preferred_element_type=f32) * score_scale
    )
    top_score = jnp.max(scores, -1, keepdims=True)
    exponent = jnp.exp(scores - top_score)
    exp_sums = jnp.sum(exponent, -1, keepdims=True)
    log_total = top_score + jnp.log(exp_sums)
    attn_probs = (exponent / exp_sums).astype(bf16)
    attended = jnp.einsum("lhqk,lkhd->lqhd", attn_probs, values_low, preferred_element_type=f32)
    attended = attended.astype(bf16).reshape(row_count, feat_width)
    attn_out = (
        reduce_features(jnp.einsum("rc,oc->ro", attended, proj_full, preferred_element_type=f32))
        + proj_bias
    )
    attn_out = attn_out.reshape(lat_shape)
    middle = field_in + gate_one * attn_out
    normed_two, inverse_two = normalize(middle)
    hidden_two = (
        (normed_two * (1.0 + scale_two) + shift_two).astype(bf16).reshape(row_count, feat_width)
    )
    full_two = gather_features(hidden_two)
    pre_act = jnp.dot(full_two, fc1_full, preferred_element_type=f32) + fc1_bias
    act_value, gelu_back = jax.vjp(partial(jax.nn.gelu, approximate=True), pre_act)
    act_low = act_value.astype(bf16)
    mlp_out = (
        reduce_features(jnp.einsum("rf,of->ro", act_low, fc2_full, preferred_element_type=f32))
        + fc2_bias
    )
    mlp_out = mlp_out.reshape(lat_shape)
    output = middle + gate_two * mlp_out
    grad_out = cotangent.T.reshape(lat_shape)
    grad_gate_two = jnp.sum(grad_out * mlp_out, 1)
    grad_mlp = (grad_out * gate_two).astype(bf16).reshape(row_count, feat_width)
    fc2_bias_grad = jnp.sum(grad_mlp, 0, dtype=f32)
    grad_mlp_full = gather_grads(grad_mlp)
    fc2_grad = jnp.einsum("ro,rf->of", grad_mlp_full, act_low, preferred_element_type=f32)
    grad_act = jnp.dot(grad_mlp_full, fc2_full, preferred_element_type=f32)
    grad_pre = gelu_back(grad_act)[0].astype(bf16)
    fc1_bias_grad = jnp.sum(grad_pre, 0, dtype=f32)
    fc1_grad = jnp.einsum("rk,rf->kf", full_two, grad_pre, preferred_element_type=f32)
    grad_hidden_two = reduce_grads(
        jnp.einsum("rf,kf->rk", grad_pre, fc1_full, preferred_element_type=f32)
    )
    grad_hidden_two = grad_hidden_two.reshape(lat_shape)
    grad_shift_two = jnp.sum(grad_hidden_two, 1)
    grad_scale_two = jnp.sum(grad_hidden_two * normed_two, 1)
    grad_middle = grad_out + norm_back(grad_hidden_two * (1.0 + scale_two), normed_two, inverse_two)
    grad_gate_one = jnp.sum(grad_middle * attn_out, 1)
    grad_attn = (grad_middle * gate_one).astype(bf16).reshape(row_count, feat_width)
    proj_bias_grad = jnp.sum(grad_attn, 0, dtype=f32)
    grad_attn_full = gather_grads(grad_attn)
    proj_grad = jnp.einsum("ro,rc->oc", grad_attn_full, attended, preferred_element_type=f32)
    grad_attended = (
        jnp.dot(grad_attn_full, proj_full, preferred_element_type=f32)
        .astype(bf16)
        .reshape(head_shape)
    )
    scores_again = (
        jnp.einsum("lqhd,lkhd->lhqk", queries, keys_low, preferred_element_type=f32) * score_scale
    )
    probs_again = jnp.exp(scores_again - log_total)
    grad_values = jnp.einsum(
        "lhqk,lqhd->lkhd", probs_again.astype(bf16), grad_attended, preferred_element_type=f32
    )
    grad_probs = jnp.einsum(
        "lqhd,lkhd->lhqk", grad_attended, values_low, preferred_element_type=f32
    )
    grad_scores = (
        probs_again * (grad_probs - jnp.sum(grad_probs * probs_again, -1, keepdims=True))
    ).astype(bf16)
    grad_queries = (
        jnp.einsum("lhqk,lkhd->lqhd", grad_scores, keys_low, preferred_element_type=f32)
        * score_scale
    )
    grad_keys = (
        jnp.einsum("lhqk,lqhd->lkhd", grad_scores, queries, preferred_element_type=f32)
        * score_scale
    )
    grad_qkv = (
        jnp.stack([grad_queries, grad_keys, grad_values])
        .astype(bf16)
        .reshape(3, row_count, feat_width)
    )
    qv_bias_grad = jnp.stack(
        [jnp.sum(grad_qkv[0], 0, dtype=f32), jnp.sum(grad_qkv[2], 0, dtype=f32)]
    )
    qkv_grad = jnp.einsum("rk,jrc->jkc", full_one, grad_qkv, preferred_element_type=f32)
    grad_hidden_one = reduce_grads(
        jnp.einsum("jrc,jkc->rk", grad_qkv, qkv_full, preferred_element_type=f32)
    )
    grad_hidden_one = grad_hidden_one.reshape(lat_shape)
    grad_shift_one = jnp.sum(grad_hidden_one, 1)
    grad_scale_one = jnp.sum(grad_hidden_one * normed_one, 1)
    tokens_grad = grad_middle + norm_back(
        grad_hidden_one * (1.0 + scale_one), normed_one, inverse_one
    )
    grad_mod = jnp.stack(
        [
            grad_shift_one,
            grad_scale_one,
            grad_gate_one,
            grad_shift_two,
            grad_scale_two,
            grad_gate_two,
        ],
        1,
    ).astype(bf16)
    ada_bias_grad = jnp.sum(grad_mod, 0, dtype=f32)
    ada_grad = jnp.einsum("lk,ljc->jkc", cond_full, grad_mod, preferred_element_type=f32)
    grad_cond_act = reduce_grads(
        jnp.einsum("ljc,jkc->lk", grad_mod, ada_full, preferred_element_type=f32)
    )
    silu_value, silu_back = jax.vjp(jax.nn.silu, condition)
    grad_condition = silu_back(grad_cond_act)[0]
    class_count = class_table.shape[1]
    one_hot = (labels[:, None] == jnp.arange(class_count, dtype=jnp.int32)[None, :]).astype(f32)
    class_grad = jnp.einsum("lc,lw->wc", one_hot, grad_condition, precision=lax.Precision.HIGHEST)
    ada_shard, qkv_shard, proj_shard, fc1_shard, fc2_shard = (
        lax.psum_scatter(ada_grad, "tok", scatter_dimension=1, tiled=True),
        lax.psum_scatter(qkv_grad, "tok", scatter_dimension=1, tiled=True),
        lax.psum_scatter(proj_grad, "tok", scatter_dimension=0, tiled=True),
        lax.psum_scatter(fc1_grad, "tok", scatter_dimension=0, tiled=True),
        lax.psum_scatter(fc2_grad, "tok", scatter_dimension=0, tiled=True),
    )
    class_sum, ada_bias_sum, qv_bias_sum, proj_bias_sum, fc1_bias_sum, fc2_bias_sum = lax.psum(
        (class_grad, ada_bias_grad, qv_bias_grad, proj_bias_grad, fc1_bias_grad, fc2_bias_grad),
        "tok",
    )
    return (
        output.reshape(row_count, feat_width).T,
        tokens_grad.reshape(row_count, feat_width).T,
        class_sum,
        ada_shard,
        ada_bias_sum,
        qkv_shard,
        qv_bias_sum,
        proj_shard,
        proj_bias_sum,
        fc1_shard,
        fc1_bias_sum,
        fc2_shard,
        fc2_bias_sum,
    )


def solution(mesh):
    return jax.shard_map(
        per_device,
        mesh=mesh,
        in_specs=(
            P("feat", "tok"),
            P("tok"),
            P("tok"),
            P("feat", None),
            P(None, "tok", "feat"),
            P(None, "feat"),
            P(None, "tok", "feat"),
            P(None, "feat"),
            P("tok", "feat"),
            P("feat"),
            P("tok", "feat"),
            P("feat"),
            P("tok", "feat"),
            P("feat"),
            P("feat", "tok"),
        ),
        out_specs=(
            P("feat", "tok"),
            P("feat", "tok"),
            P("feat", None),
            P(None, "tok", "feat"),
            P(None, "feat"),
            P(None, "tok", "feat"),
            P(None, "feat"),
            P("tok", "feat"),
            P("feat"),
            P("tok", "feat"),
            P("feat"),
            P("tok", "feat"),
            P("feat"),
        ),
        check_vma=False,
    )
```

profile of v0, /device:TPU:0, one launch (start us, length us, event | category | flops | bytes accessed | tf_op | source)
XLA Modules:
  0.0 819.7 jit_solution(17408276316138479012)
XLA Ops:
  13.3 6.0 all-gather
  19.4 32.8 %all_gather.34 = bf16[768,192]{1,0:T(8,128)(2,1)S(1)} all-gather(bf16[96,192]{1,0:T(8,128)(2,1)S(1)} %copy-done.34), channel_id=1, replica_groups=mesh['tok'=8,'feat'=4] {'tok'}, dimensions={0}, use_global_device_ids=true | all-gather | bytes 331776 | tf_op jit(solution)/shard_map/all_gather | solution.py:89
  52.4 41.3 %all_gather.33 = bf16[3,768,192]{2,0,1:T(4,128)(2,1)S(1)} all-gather(bf16[3,96,192]{2,0,1:T(4,128)(2,1)S(1)} %copy.81), channel_id=1, replica_groups=mesh['tok'=8,'feat'=4] {'tok'}, dimensions={1}, use_global_device_ids=true | all-gather | bytes 995328 | tf_op jit(solution)/shard_map/all_gather | solution.py:88
  93.7 2.1 copy.82
  95.8 6.1 psum.98
  102.6 6.5 psum.99
  110.4 2.1 convolution_add_fusion.1
  114.1 8.2 all_gather.32
  140.3 11.2 %all_gather.38 = bf16[512,768]{0,1:T(8,128)(2,1)} all-gather(bf16[512,192]{0,1:T(8,128)(2,1)} %get-tuple-element.74), channel_id=1, replica_groups=mesh['tok'=8,'feat'=4] {'feat'}, dimensions={1}, use_global_device_ids=true | all-gather | bytes 983040 | tf_op jit(solution)/shard_map/all_gather | solution.py:42
  151.5 3.5 fusion.59
  155.0 3.7 reduce-scatter.17.cloned.1.call-done
  158.7 2.0 fusion.55
  160.8 6.3 psum.100
  167.8 5.7 psum.101
  175.1 9.0 %all_gather.35 = bf16[512,768]{0,1:T(8,128)(2,1)} all-gather(bf16[512,192]{0,1:T(8,128)(2,1)S(1)} %add_convert_fusion), channel_id=1, replica_groups=mesh['tok'=8,'feat'=4] {'feat'}, dimensions={1}, use_global_device_ids=true | all-gather | bytes 983040 | tf_op jit(solution)/shard_map/all_gather | solution.py:38
  184.1 17.3 %all-gather.7.cloned.1.call-done = bf16[768,768]{1,0:T(8,128)(2,1)} async-done(((bf16[96,768]{1,0:T(8,128)(2,1)}), bf16[768,768]{1,0:T(8,128)(2,1)}) %all-gather.7.cloned.1.call-update) | async-done | bytes 1179664 | tf_op jit(solution)/shard_map/all_gather | solution.py:90
  201.4 5.6 convert_reduce_fusion
  210.4 21.4 %reduce-scatter.21.cloned.1.call-done = bf16[512,192]{0,1:T(8,128)(2,1)} async-done(((bf16[512,768]{0,1:T(8,128)(2,1)}), bf16[512,192]{0,1:T(8,128)(2,1)}) %reduce-scatter.21.cloned.1.call-update) | async-done | bytes 196624 | tf_op jit(solution)/shard_map/reduce_scatter | solution.py:50
  236.0 6.6 all-reduce.2
  244.6 2.0 convert_reduce_fusion.4
  246.6 8.7 %all_gather.39 = bf16[512,768]{0,1:T(8,128)(2,1)S(1)} all-gather(bf16[512,192]{0,1:T(8,128)(2,1)S(1)} %get-tuple-element.78), channel_id=1, replica_groups=mesh['tok'=8,'feat'=4] {'feat'}, dimensions={1}, use_global_device_ids=true | all-gather | bytes 983040 | tf_op jit(solution)/shard_map/all_gather | solution.py:42
  267.1 1.8 copy.96
  268.9 1.7 stack.58
  270.6 1.8 copy.99
  272.4 1.7 stack.59
  277.8 3.9 fusion.53
  283.8 2.0 reshape.196
  286.8 14.4 %reduce-scatter.23.cloned.1.call-done = bf16[512,192]{0,1:T(8,128)(2,1)} async-done(((bf16[512,768]{0,1:T(8,128)(2,1)}), bf16[512,192]{0,1:T(8,128)(2,1)}) %reduce-scatter.23.cloned.1.call-update) | async-done | bytes 196624 | tf_op jit(solution)/shard_map/reduce_scatter | solution.py:50
  302.3 6.3 all-reduce.1
  309.2 22.9 %reduce-scatter.19.cloned.1.call-done = f32[512,192]{0,1:T(8,128)} async-done(((f32[512,768]{0,1:T(8,128)}), f32[512,192]{0,1:T(8,128)}) %reduce-scatter.19.cloned.1.call-update) | async-done | bytes 393232 | tf_op jit(solution)/shard_map/reduce_scatter | solution.py:46
  332.1 2.3 add_bitcast_fusion.1
  334.4 2.0 reshape.197
  337.5 5.3 multiply_reduce_fusion.2
  349.8 2.9 convolution_bitcast_fusion.1
  352.8 3.0 copy.117
  355.7 2.8 reshape.223
  359.9 4.1 copy.115
  364.0 6.6 reshape.221
  375.7 2.3 fusion.61
  379.6 2.3 fusion.52
  382.8 37.9 %all-reduce = (f32[6,192]{1,0:T(8,128)}, f32[2,192]{1,0:T(2,128)}, f32[192]{0:T(256)}, f32[768]{0:T(1024)}, f32[192]{0:T(256)}) all-reduce(f32[6,192]{1,0:T(8,128)S(1)} %convert_reduce_fusion.5, f32[2,192]{1,0:T(2,128)S(1)} %pad_maximum_fusion, f32[192]{0:T(256)S(1)} %copy-done.53, ...), channel_id=1, replica_groups=mesh['tok'=8,'feat'=4] {'tok'}, use_global_device_ids=true, to_apply=%region_33.34 | all-reduce | flops 2688 | bytes 21504 | tf_op jit(solution)/shard_map/psum | solution.py:236
  420.7 19.4 %reduce-scatter.35.cloned.1.call-done = f32[96,576]{1,0:T(8,128)} async-done(((f32[768,576]{1,0:T(8,128)}), f32[96,576]{1,0:T(8,128)}) %reduce-scatter.35.cloned.1.call-update) | async-done | bytes 221200
  442.0 80.2 %reduce-scatter.33.cloned.1.call-done = f32[96,1152]{1,0:T(8,128)} async-done(((f32[768,1152]{1,0:T(8,128)}), f32[96,1152]{1,0:T(8,128)}) %reduce-scatter.33.cloned.1.call-update) | async-done | bytes 442384
  524.5 64.1 %reduce-scatter.25.cloned.1.call-done = f32[96,192]{1,0:T(8,128)} async-done(((f32[768,192]{1,0:T(8,128)}), f32[96,192]{1,0:T(8,128)}) %reduce-scatter.25.cloned.1.call-update) | async-done | bytes 73744 | tf_op jit(solution)/shard_map/reduce_scatter | solution.py:232
  588.5 77.5 %all-reduce.5.cloned.1.call-done = f32[192,1001]{1,0:T(8,128)} async-done(((f32[192,1001]{1,0:T(8,128)}), f32[192,1001]{1,0:T(8,128)}) %all-reduce.5.cloned.1.call-update) | async-done | bytes 768784 | tf_op jit(solution)/shard_map/psum | solution.py:236
  666.1 72.6 %reduce-scatter.27.cloned.1.call-done = f32[96,768]{1,0:T(8,128)} async-done(((f32[768,768]{1,0:T(8,128)}), f32[96,768]{1,0:T(8,128)}) %reduce-scatter.27.cloned.1.call-update) | async-done | bytes 294928 | tf_op jit(solution)/shard_map/reduce_scatter | solution.py:233
  738.7 72.4 %reduce-scatter.29.cloned.1.call-done = f32[96,768]{1,0:T(8,128)} async-done(((f32[768,768]{1,0:T(8,128)}), f32[96,768]{1,0:T(8,128)}) %reduce-scatter.29.cloned.1.call-update) | async-done | bytes 294928 | tf_op jit(solution)/shard_map/reduce_scatter | solution.py:234
  811.1 2.1 copy.179
  (272 shorter events, 80.6 us)
Async XLA Ops:
  7.2 12.2 %copy-start.34 = (bf16[96,192]{1,0:T(8,128)(2,1)S(1)}, bf16[96,192]{1,0:T(8,128)(2,1)}, u32[]{:S(2)}) copy-start(bf16[96,192]{1,0:T(8,128)(2,1)} %param.23) | copy-start | bytes 110596
  7.2 45.1 %copy-start.30 = (bf16[3,96,192]{2,1,0:T(8,128)(2,1)S(1)}, bf16[3,96,192]{2,1,0:T(8,128)(2,1)}, u32[]{:S(2)}) copy-start(bf16[3,96,192]{2,1,0:T(8,128)(2,1)} %param.21) | copy-start | bytes 331780
  7.2 103.2 %all-gather.5.cloned.1.call-start = ((), (), s32[]{:S(2)}) async-start(), calls=%async_computation.10 | async-start | bytes 2654208 | tf_op jit(solution)/shard_map/all_gather | solution.py:87
  7.9 143.6 %all-gather.9.cloned.1.call-start = ((), (), s32[]{:S(2)}) async-start(), calls=%async_computation.13 | async-start | bytes 1327104 | tf_op jit(solution)/shard_map/all_gather | solution.py:91
  8.7 150.1 %reduce-scatter.17.cloned.1.call-start = ((), (), s32[]{:S(2)}) async-start(), calls=%async_computation.11 | async-start | bytes 1966080 | tf_op jit(solution)/shard_map/reduce_scatter | solution.py:46
  19.4 91.0 %copy-start.38 = (bf16[768,2,1]{0,1,2:T(2,128)(2,1)}, bf16[768,2,1]{0,1,2:T(2,128)(2,1)S(1)}, u32[]{:S(2)}) copy-start(bf16[768,2,1]{0,1,2:T(2,128)(2,1)S(1)} %reshape.212) | copy-start | bytes 9220
  52.2 77.1 %copy-start.14 = (bf16[768,192]{1,0:T(8,128)(2,1)}, bf16[768,192]{1,0:T(8,128)(2,1)S(1)}, u32[]{:S(2)}) copy-start(bf16[768,192]{1,0:T(8,128)(2,1)S(1)} %all_gather.34) | copy-start | bytes 884740
  93.7 15.9 %copy-start.56 = (f32[2,192]{1,0:T(2,128)S(1)}, f32[2,192]{1,0:T(2,128)}, u32[]{:S(2)}) copy-start(f32[2,192]{1,0:T(2,128)} %param.22) | copy-start | bytes 4612
  93.7 16.7 %copy-start.44 = (f32[6,192]{1,0:T(8,128)S(1)}, f32[6,192]{1,0:T(8,128)}, u32[]{:S(2)}) copy-start(f32[6,192]{1,0:T(8,128)} %param.20) | copy-start | bytes 13828
  109.6 4.3 copy-start.35
  109.7 17.0 %copy-start.40 = (f32[3,64]{1,0:T(4,128)}, f32[3,64]{1,0:T(4,128)S(1)}, u32[]{:S(2)}) copy-start(f32[3,64]{1,0:T(4,128)S(1)} %add.215) | copy-start | bytes 2308
  113.9 8.4 %copy-start.8 = (bf16[3,768,192]{1,2,0:T(8,128)(2,1)S(1)}, bf16[3,768,192]{1,2,0:T(8,128)(2,1)}, u32[]{:S(2)}) copy-start(bf16[3,768,192]{1,2,0:T(8,128)(2,1)} %copy.82) | copy-start | bytes 2654212
  114.0 9.0 %copy-start.6 = (f32[24,8,2,256]{3,1,2,0:T(8,128)}, f32[24,8,2,256]{3,1,2,0:T(8,128)S(1)}, u32[]{:S(2)}) copy-start(f32[24,8,2,256]{3,1,2,0:T(8,128)S(1)} %copy.124) | copy-start | bytes 1179652
  125.7 2.7 copy-start.12
  131.5 2.5 copy-start.51
  131.5 69.9 %all-gather.7.cloned.1.call-start = ((), (), s32[]{:S(2)}) async-start(), calls=%async_computation.12 | async-start | bytes 1327104 | tf_op jit(solution)/shard_map/all_gather | solution.py:90
  132.1 99.7 %reduce-scatter.21.cloned.1.call-start = ((), (), s32[]{:S(2)}) async-start(), calls=%async_computation.15 | async-start | bytes 983040 | tf_op jit(solution)/shard_map/reduce_scatter | solution.py:50
  132.6 4.2 copy-start.50
  132.6 6.9 copy-start.10
  134.1 5.4 copy-start.49
  151.5 7.2 copy-start.57
  174.0 33.0 %copy-start.32 = (f32[1,2,2,128]{3,1,2,0:T(2,128)}, f32[1,2,2,128]{3,1,2,0:T(2,128)S(1)}, u32[]{:S(2)}) copy-start(f32[1,2,2,128]{3,1,2,0:T(2,128)S(1)} %copy.129) | copy-start | bytes 6148
  201.4 6.5 copy-start.59
  209.6 91.7 %reduce-scatter.23.cloned.1.call-start = ((), (), s32[]{:S(2)}) async-start(), calls=%async_computation.16 | async-start | bytes 983040 | tf_op jit(solution)/shard_map/reduce_scatter | solution.py:50
  242.6 13.7 %copy-start.15 = (bf16[768,192]{1,0:T(8,128)(2,1)S(1)}, bf16[768,192]{1,0:T(8,128)(2,1)}, u32[]{:S(2)}) copy-start(bf16[768,192]{1,0:T(8,128)(2,1)} %copy-done.14) | copy-start | bytes 884740
  243.3 12.1 %copy-start.42 = (f32[1,2,2,128]{3,1,2,0:T(2,128)}, f32[1,2,2,128]{3,1,2,0:T(2,128)S(1)}, u32[]{:S(2)}) copy-start(f32[1,2,2,128]{3,1,2,0:T(2,128)S(1)} %copy.133) | copy-start | bytes 6148
  244.6 10.8 %copy-start.43 = (f32[1,2,2,128]{3,1,2,0:T(2,128)}, f32[1,2,2,128]{3,1,2,0:T(2,128)S(1)}, u32[]{:S(2)}) copy-start(f32[1,2,2,128]{3,1,2,0:T(2,128)S(1)} %copy.132) | copy-start | bytes 6148
  265.3 10.7 %copy-start.9 = (bf16[3,768,192]{1,2,0:T(8,128)(2,1)S(1)}, bf16[3,768,192]{1,2,0:T(8,128)(2,1)}, u32[]{:S(2)}) copy-start(bf16[3,768,192]{1,2,0:T(8,128)(2,1)} %copy.82) | copy-start | bytes 2654212
  277.8 54.4 %reduce-scatter.19.cloned.1.call-start = ((), (), s32[]{:S(2)}) async-start(), calls=%async_computation.14 | async-start | bytes 1966080 | tf_op jit(solution)/shard_map/reduce_scatter | solution.py:46
  281.8 4.1 copy-start.16
  281.8 19.5 %copy-start.7 = (f32[24,8,2,256]{3,1,2,0:T(8,128)S(1)}, f32[24,8,2,256]{3,1,2,0:T(8,128)}, u32[]{:S(2)}) copy-start(f32[24,8,2,256]{3,1,2,0:T(8,128)} %copy-done.6) | copy-start | bytes 1179652
  281.8 19.5 %copy-start.36 = (f32[1,2,2,128]{3,1,2,0:T(2,128)S(1)}, f32[1,2,2,128]{3,1,2,0:T(2,128)}, u32[]{:S(2)}) copy-start(f32[1,2,2,128]{3,1,2,0:T(2,128)} %copy-done.35) | copy-start | bytes 6148
  281.8 91.3 %reduce-scatter.31.cloned.1.call-start = ((), (), s32[]{:S(2)}) async-start(), calls=%async_computation.21 | async-start | bytes 245760
  282.8 49.3 %copy-start.11 = (f32[24,8,2,256]{3,1,2,0:T(8,128)S(1)}, f32[24,8,2,256]{3,1,2,0:T(8,128)}, u32[]{:S(2)}) copy-start(f32[24,8,2,256]{3,1,2,0:T(8,128)} %copy-done.10) | copy-start | bytes 1179652
  282.8 49.3 %copy-start.33 = (f32[1,2,2,128]{3,1,2,0:T(2,128)S(1)}, f32[1,2,2,128]{3,1,2,0:T(2,128)}, u32[]{:S(2)}) copy-start(f32[1,2,2,128]{3,1,2,0:T(2,128)} %copy-done.32) | copy-start | bytes 6148
  332.1 4.3 copy-start.19
  334.4 3.0 copy-start.24
  337.5 10.7 %copy-start.1 = (bf16[6,768,192]{2,1,0:T(8,128)(2,1)S(1)}, bf16[6,768,192]{2,1,0:T(8,128)(2,1)}, u32[]{:S(2)}) copy-start(bf16[6,768,192]{2,1,0:T(8,128)(2,1)} %all-gather.5.cloned.1.call-done) | copy-start | bytes 5308420
  349.8 90.3 %reduce-scatter.35.cloned.1.call-start = ((), (), s32[]{:S(2)}) async-start(), calls=%async_computation.23 | async-start | bytes 2211840
  358.6 163.6 %reduce-scatter.33.cloned.1.call-start = ((), (), s32[]{:S(2)}) async-start(), calls=%async_computation.22 | async-start | bytes 3981312
  370.6 3.5 copy-start.48
  370.6 3.5 copy-start.58
  370.7 217.9 %reduce-scatter.25.cloned.1.call-start = ((), (), s32[]{:S(2)}) async-start(), calls=%async_computation.18 | async-start | bytes 884736 | tf_op jit(solution)/shard_map/reduce_scatter | solution.py:232
  373.0 2.6 copy-start.17
  373.0 2.6 copy-start.29
  373.0 293.0 %all-reduce.5.cloned.1.call-start = ((), (), s32[]{:S(2)}) async-start(), calls=%async_computation.17 | async-start | bytes 1572864 | tf_op jit(solution)/shard_map/psum | solution.py:236
  375.6 363.1 %reduce-scatter.27.cloned.1.call-start = ((), (), s32[]{:S(2)}) async-start(), calls=%async_computation.19 | async-start | bytes 2654208 | tf_op jit(solution)/shard_map/reduce_scatter | solution.py:233
  378.0 433.1 %reduce-scatter.29.cloned.1.call-start = ((), (), s32[]{:S(2)}) async-start(), calls=%async_computation.20 | async-start | bytes 2654208 | tf_op jit(solution)/shard_map/reduce_scatter | solution.py:234
  (27 other events, 32.4 us)
Sparse Core Ops, SparseCore 0:
  10.2 74.3 all-gather.4
  86.8 41.7 all-gather.8
  131.6 27.0 reduce-scatter.16
  161.0 40.3 all-gather.6
  209.7 22.0 reduce-scatter.20
  277.9 23.3 reduce-scatter.22
  304.0 28.1 reduce-scatter.18
  349.9 19.7 reduce-scatter.30
  373.1 66.9 reduce-scatter.34
  444.0 78.0 reduce-scatter.32
  526.4 62.1 reduce-scatter.24
  592.4 73.6 all-reduce.4
  670.6 68.1 reduce-scatter.26
  743.0 68.0 reduce-scatter.28
where the time goes:
time: 822 us; the launch traced here: 820 us
  waiting for transfers between devices  468 us (57%)
  blocking collectives  193 us (23%)
  local copies, waits for them, and re-layouts  77.9 us (9%)
  matrix products  40.2 us (5%)
  other arithmetic  25.6 us (3%)
  between operations  14.6 us (2%)
    unnamed x17, waiting for transfers between devices  102 us
    psum x1, waiting for transfers between devices, per_device(): lax.psum((class_grad, ada_bias_grad, qv_bias_grad, proj_bias_grad, fc1_bi...  77.5 us
    reduce_scatter x1, waiting for transfers between devices, per_device(): lax.psum_scatter(fc1_grad, 'tok', scatter_dimension=0, tiled=True)  72.6 us
    reduce_scatter x1, waiting for transfers between devices, per_device(): lax.psum_scatter(fc2_grad, 'tok', scatter_dimension=0, tiled=True)  72.4 us
    reduce_scatter x1, waiting for transfers between devices, per_device(): lax.psum_scatter(proj_grad, 'tok', scatter_dimension=0, tiled=True)  64.1 us
    unnamed x163, local copies, waits for them, and re-layouts  43.6 us
    all_gather x1, blocking collectives, per_device(): lax.all_gather(qkv_weight, 'tok', axis=1, tiled=True)  41.3 us
    psum x1, blocking collectives, per_device(): lax.psum((class_grad, ada_bias_grad, qv_bias_grad, proj_bias_grad, fc1_bi...  37.9 us
  transfers between devices with their start and end apart: 14, of which 11 were waited for; matrix products, arithmetic and copies ran while one was open for 10% of the time, Pallas kernels for 0%

commit v1 on v0

v1 whole, which is shorter than its diff:
```python
from functools import partial
import math

import jax
import jax.numpy as jnp
from jax import lax
from jax.experimental import pallas as pl
from jax.experimental.pallas import tpu as pltpu
from jax.sharding import PartitionSpec as P

D = 768
HEAD_DIM = 64
FEAT = 4
MESH = pl.DeviceIdType.MESH
F32 = jnp.float32
BF16 = jnp.bfloat16
VMEM = pl.BlockSpec(memory_space=pltpu.VMEM)


def time_features(step_ids, feat_count):
    half_width = feat_count // 2
    frequency = jnp.exp(-math.log(10000.0) * jnp.arange(half_width, dtype=jnp.float32) / half_width)
    angles = step_ids.astype(jnp.float32)[:, None] * frequency[None, :]
    return jnp.concatenate([jnp.cos(angles), jnp.sin(angles)], axis=-1)


def partners():
    f = lax.axis_index("feat")
    near = f + 1 - 2 * (f % 2)
    far = (f + 2) % FEAT
    return f, near, far, (near + 2) % FEAT


def greet(near, far, cross):
    barrier = pltpu.get_barrier_semaphore()
    for peer in (near, far, cross):
        pl.semaphore_signal(barrier, inc=1, device_id={"feat": peer}, device_id_type=MESH)
    pl.semaphore_wait(barrier, 3)


def push(src, dst, sems, at, peer):
    return pltpu.make_async_remote_copy(
        src_ref=src,
        dst_ref=dst,
        send_sem=sems.at[0, at],
        recv_sem=sems.at[1, at],
        device_id={"feat": peer},
        device_id_type=MESH,
    )


def gather_start(buf, sems, base):
    f, near, far, _ = partners()
    to_far = push(buf.at[f], buf.at[f], sems, base, far)
    to_near = push(buf.at[f], buf.at[f], sems, base + 1, near)
    to_far.start()
    to_near.start()
    return to_far, to_near


def gather_forward(buf, sems, base, started):
    _, near, far, _ = partners()
    started[0].wait_recv()
    relay = push(buf.at[far], buf.at[far], sems, base + 2, near)
    relay.start()
    return relay


def gather_finish(buf, out, started, relay):
    started[1].wait_recv()
    relay.wait_recv()
    for copy in (*started, relay):
        copy.wait_send()
    width = buf.shape[2]
    for block in range(FEAT):
        out[:, block * width : (block + 1) * width] = buf[block]


def scatter_start(term, buf, near_in, sems, base):
    f, near, _, _ = partners()
    side, core = f // 2, f % 2
    width = buf.shape[2]
    for block in range(FEAT):
        buf[block] = term[:, block * width : (block + 1) * width]
    first = push(buf.at[2 * (1 - side) + 1 - core], near_in.at[0], sems, base, near)
    second = push(buf.at[2 * side + 1 - core], near_in.at[1], sems, base + 1, near)
    first.start()
    second.start()
    return first, second


def scatter_cross(buf, near_in, out_buf, far_in, sems, base, started):
    _, _, far, _ = partners()
    started[0].wait_recv()
    out_buf[...] = (buf[far].astype(F32) + near_in[0].astype(F32)).astype(BF16)
    cross = push(out_buf, far_in, sems, base + 2, far)
    cross.start()
    return cross


def scatter_finish(buf, near_in, far_in, started, cross):
    f, _, _, _ = partners()
    started[1].wait_recv()
    own = buf[f].astype(F32) + near_in[1].astype(F32)
    cross.wait_recv()
    for copy in (*started, cross):
        copy.wait_send()
    return own + far_in[...].astype(F32)


def swap_rows(pair, stats, sems, base):
    _, near, far, cross = partners()
    rows = pair[0].shape[0]
    lane = lax.broadcasted_iota(jnp.int32, (rows, 128), 1)
    packed = jnp.where(lane == 0, pair[0], jnp.where(lane == 1, pair[1], 0.0))
    stats[0] = packed.T[:8]
    copies = [
        push(stats.at[0], stats.at[slot], sems, base + slot - 1, peer)
        for slot, peer in ((1, near), (2, far), (3, cross))
    ]
    for copy in copies:
        copy.start()
    for copy in copies:
        copy.wait()
    return stats[...]


def columns(first, second):
    rows = first.shape[1]
    tall = jnp.concatenate([first, second, jnp.zeros((126, rows), F32)], 0).T
    return tall[:, 0:1], tall[:, 1:2]


def norm_stats(values, stats, sems, base):
    width = values.shape[1]
    local = jnp.sum(values, 1, keepdims=True)
    off = values - local / width
    got = swap_rows((local, jnp.sum(off * off, 1, keepdims=True)), stats, sems, base)
    sums, squares = got[:, 0], got[:, 1]
    mean = jnp.sum(sums, 0, keepdims=True) / D
    shifted = sums / width - mean
    variance = jnp.sum(squares + width * shifted * shifted, 0, keepdims=True) / D
    return columns(mean, lax.rsqrt(variance + 1e-06))


def norm_grad(grad_norm, normed, inverse, stats, sems, base):
    got = swap_rows(
        (jnp.sum(grad_norm, 1, keepdims=True), jnp.sum(grad_norm * normed, 1, keepdims=True)),
        stats,
        sems,
        base,
    )
    total = jnp.sum(got, 0)
    first, second = columns(total[0:1] / D, total[1:2] / D)
    return inverse * (grad_norm - first - normed * second)


def spread(mod, which, rows):
    count = mod.shape[0] // 6
    return jnp.concatenate(
        [
            jnp.broadcast_to(mod[l * 6 + which : l * 6 + which + 1], (rows // count, mod.shape[1]))
            for l in range(count)
        ],
        0,
    )


def latent_sums(out, values, which, kinds):
    count = out.shape[0] // kinds
    seq = values.shape[0] // count
    for l in range(count):
        row = l * kinds + which
        out[row : row + 1] = jnp.sum(values[l * seq : (l + 1) * seq], 0, keepdims=True)


def open_kernel(x, mod, grad_out, full, grad_full, normed_out, inverse_out, fc2_sum, buf, grad_buf, stats, sems):
    f, near, far, cross = partners()
    rows = x.shape[0]
    mods = mod[...]
    greet(near, far, cross)
    grad_mlp = (grad_out[...] * spread(mods, 5, rows)).astype(BF16)
    fc2_sum[...] = jnp.sum(grad_mlp.astype(F32), 0, keepdims=True)
    grad_buf[f] = grad_mlp
    values = x[...]
    mean, inverse = norm_stats(values, stats, sems, 0)
    normed = (values - mean) * inverse
    normed_out[...] = normed
    inverse_out[...] = inverse
    buf[f] = (normed * (1.0 + spread(mods, 1, rows)) + spread(mods, 0, rows)).astype(BF16)
    started = gather_start(buf, sems, 3)
    grad_started = gather_start(grad_buf, sems, 6)
    relay = gather_forward(buf, sems, 3, started)
    gather_finish(buf, full, started, relay)
    grad_relay = gather_forward(grad_buf, sems, 6, grad_started)
    gather_finish(grad_buf, grad_full, grad_started, grad_relay)


def middle_kernel(
    term, x, mod, bias, attn_out, middle_out, normed_out, inverse_out, full,
    sbuf, near_in, out_buf, far_in, buf, stats, sems,
):
    f, near, far, cross = partners()
    rows = x.shape[0]
    mods = mod[...]
    greet(near, far, cross)
    started = scatter_start(term, sbuf, near_in, sems, 0)
    crossing = scatter_cross(sbuf, near_in, out_buf, far_in, sems, 0, started)
    attn = scatter_finish(sbuf, near_in, far_in, started, crossing) + bias[...]
    attn_out[...] = attn
    middle = x[...] + spread(mods, 2, rows) * attn
    middle_out[...] = middle
    mean, inverse = norm_stats(middle, stats, sems, 3)
    normed = (middle - mean) * inverse
    normed_out[...] = normed
    inverse_out[...] = inverse
    buf[f] = (normed * (1.0 + spread(mods, 4, rows)) + spread(mods, 3, rows)).astype(BF16)
    gathering = gather_start(buf, sems, 6)
    relay = gather_forward(buf, sems, 6, gathering)
    gather_finish(buf, full, gathering, relay)


def back_kernel(
    term, mlp_term, grad_out, normed_in, inverse_in, mod, bias, middle, attn,
    grad_middle_out, full, output, sums, proj_sum,
    sbuf, near_in, out_buf, far_in, mbuf, mnear, mout, mfar, buf, stats, sems,
):
    f, near, far, cross = partners()
    rows = grad_out.shape[0]
    mods = mod[...]
    greet(near, far, cross)
    started = scatter_start(term, sbuf, near_in, sems, 0)
    mlp_started = scatter_start(mlp_term, mbuf, mnear, sems, 3)
    crossing = scatter_cross(sbuf, near_in, out_buf, far_in, sems, 0, started)
    grad_hidden = scatter_finish(sbuf, near_in, far_in, started, crossing)
    normed = normed_in[...]
    grad_middle = grad_out[...] + norm_grad(
        grad_hidden * (1.0 + spread(mods, 4, rows)), normed, inverse_in[...], stats, sems, 6
    )
    grad_attn = (grad_middle * spread(mods, 2, rows)).astype(BF16)
    buf[f] = grad_attn
    gathering = gather_start(buf, sems, 9)
    mlp_crossing = scatter_cross(mbuf, mnear, mout, mfar, sems, 3, mlp_started)
    grad_middle_out[...] = grad_middle
    proj_sum[...] = jnp.sum(grad_attn.astype(F32), 0, keepdims=True)
    latent_sums(sums, grad_hidden, 0, 4)
    latent_sums(sums, grad_hidden * normed, 1, 4)
    latent_sums(sums, grad_middle * attn[...], 2, 4)
    relay = gather_forward(buf, sems, 9, gathering)
    gather_finish(buf, full, gathering, relay)
    mlp_out = scatter_finish(mbuf, mnear, mfar, mlp_started, mlp_crossing) + bias[...]
    output[...] = middle[...] + spread(mods, 5, rows) * mlp_out
    latent_sums(sums, grad_out[...] * mlp_out, 3, 4)


def close_kernel(
    term, normed_in, inverse_in, mod, grad_middle, tokens_grad, sums,
    sbuf, near_in, out_buf, far_in, stats, sems,
):
    _, near, far, cross = partners()
    rows = normed_in.shape[0]
    mods = mod[...]
    greet(near, far, cross)
    started = scatter_start(term, sbuf, near_in, sems, 0)
    crossing = scatter_cross(sbuf, near_in, out_buf, far_in, sems, 0, started)
    grad_hidden = scatter_finish(sbuf, near_in, far_in, started, crossing)
    normed = normed_in[...]
    tokens_grad[...] = grad_middle[...] + norm_grad(
        grad_hidden * (1.0 + spread(mods, 1, rows)), normed, inverse_in[...], stats, sems, 3
    )
    latent_sums(sums, grad_hidden, 0, 2)
    latent_sums(sums, grad_hidden * normed, 1, 2)


def mod_kernel(count, term, bias, out, recv, sems):
    t = lax.axis_index("tok")
    barrier = pltpu.get_barrier_semaphore()
    for step in range(1, count):
        pl.semaphore_signal(
            barrier, inc=1, device_id={"tok": (t + step) % count}, device_id_type=MESH
        )
    pl.semaphore_wait(barrier, count - 1)
    copies = []
    for step in range(1, count):
        peer = (t + step) % count
        copies.append(
            pltpu.make_async_remote_copy(
                src_ref=term.at[peer],
                dst_ref=recv.at[step - 1],
                send_sem=sems.at[0, step - 1],
                recv_sem=sems.at[1, step - 1],
                device_id={"tok": peer},
                device_id_type=MESH,
            )
        )
    for copy in copies:
        copy.start()
    for copy in copies:
        copy.wait()
    out[...] = term[t] + jnp.sum(recv[...], 0) + bias[...]


def call(kernel, collective_id, outs, scratch, sem_count, *args):
    out_shape = [jax.ShapeDtypeStruct(shape, dtype) for shape, dtype in outs]
    return pl.pallas_call(
        kernel,
        out_shape=out_shape,
        in_specs=[VMEM] * len(args),
        out_specs=[VMEM] * len(outs),
        scratch_shapes=[pltpu.VMEM(shape, dtype) for shape, dtype in scratch]
        + [pltpu.SemaphoreType.DMA((2, sem_count))],
        compiler_params=pltpu.CompilerParams(
            collective_id=collective_id, has_side_effects=True, vmem_limit_bytes=40 * 2**20
        ),
    )(*args)


def bits_of(count):
    return [count >> (i + 1) for i in range(count.bit_length() - 1)]


def pick(values, axis, at):
    return jnp.where(
        at == 0, lax.index_in_dim(values, 0, axis, False), lax.index_in_dim(values, 1, axis, False)
    )


def gather_rows(block, row_axis, count, order):
    t = lax.axis_index("tok")
    bits = bits_of(count)
    seen = []
    held = block
    for bit in [bits[i] for i in order]:
        other = lax.ppermute(held, "tok", [(i, i ^ bit) for i in range(count)])
        axis = row_axis + sum(1 for b in seen if b > bit)
        low = (t // bit) % 2 == 0
        held = jnp.stack(
            [jnp.where(low, held, other), jnp.where(low, other, held)], axis
        )
        seen.append(bit)
    shape = list(block.shape)
    shape[row_axis] *= count
    return held.reshape(shape)


def scatter_rows(grad, row_axis, count, order):
    t = lax.axis_index("tok")
    bits = bits_of(count)
    shape = list(grad.shape)
    rows = shape[row_axis] // count
    held = grad.reshape(shape[:row_axis] + [2] * len(bits) + [rows] + shape[row_axis + 1 :])
    left = list(bits)
    for bit in [bits[i] for i in order]:
        axis = row_axis + left.index(bit)
        mine = (t // bit) % 2
        sent = pick(held, axis, 1 - mine).astype(BF16)
        got = lax.ppermute(sent, "tok", [(i, i ^ bit) for i in range(count)])
        held = pick(held, axis, mine).astype(F32) + got.astype(F32)
        left.remove(bit)
    return held


def per_device(
    tok_count,
    tokens,
    timesteps,
    labels,
    class_table,
    ada_weight,
    ada_bias,
    qkv_weight,
    qv_bias,
    proj_weight,
    proj_bias,
    fc1_weight,
    fc1_bias,
    fc2_weight,
    fc2_bias,
    cotangent,
):
    width, rows = tokens.shape
    lat = timesteps.shape[0]
    seq_len = rows // lat
    head_count = width // HEAD_DIM
    score_scale = HEAD_DIM ** (-0.5)
    feat_at, tok_at = lax.axis_index("feat"), lax.axis_index("tok")
    offset = feat_at * width
    head_shape = (lat, seq_len, head_count, HEAD_DIM)
    part = ada_weight.shape[1]
    levels = len(bits_of(tok_count))
    down = list(range(levels))
    mixed = [levels - 1] + list(range(levels - 1))

    waves = lax.dynamic_slice_in_dim(time_features(timesteps, D), offset, width, 1)
    condition = jnp.take(class_table, labels, axis=1).T.astype(F32) + waves
    cond_all = lax.all_gather(condition, ("tok", "feat"), axis=0, tiled=False)
    cond_all = (
        cond_all.reshape(tok_count, FEAT, lat, width)
        .transpose(0, 2, 1, 3)
        .reshape(tok_count * lat, D)
    )
    labels_all = lax.all_gather(labels, "tok", axis=0, tiled=True)
    qkv_full = gather_rows(qkv_weight, 1, tok_count, down)
    proj_full = gather_rows(proj_weight, 0, tok_count, mixed)
    fc1_full = gather_rows(fc1_weight, 0, tok_count, mixed)
    fc2_full = gather_rows(fc2_weight, 0, tok_count, down)

    cond_rows = jax.nn.silu(
        lax.dynamic_slice_in_dim(cond_all, tok_at * part, part, 1)
    ).astype(BF16)
    mod_term = jnp.einsum("lk,jkc->ljc", cond_rows, ada_weight, preferred_element_type=F32)
    mod_term = mod_term.reshape(tok_count, lat * 6, width)
    (mod,) = call(
        partial(mod_kernel, tok_count),
        0,
        [((lat * 6, width), F32)],
        [((tok_count - 1, lat * 6, width), F32)],
        tok_count - 1,
        mod_term,
        jnp.tile(ada_bias, (lat, 1)),
    )

    own_f32 = ((rows, width), F32)
    own_low = ((rows, width), BF16)
    one_f32 = ((rows, 1), F32)
    full_low = ((rows, D), BF16)
    line = ((1, width), F32)
    buf = ((FEAT, rows, width), BF16)
    stats = ((FEAT, 8, rows), F32)
    scatter_bufs = [buf, ((2, rows, width), BF16), own_low, own_low]

    field_in = tokens.T
    grad_out = cotangent.T
    full_one, grad_mlp_full, normed_one, inverse_one, fc2_bias_grad = call(
        open_kernel,
        1,
        [full_low, full_low, own_f32, one_f32, line],
        [buf, buf, stats],
        9,
        field_in,
        mod,
        grad_out,
    )
    projected = jnp.einsum("rk,jkc->jrc", full_one, qkv_full, preferred_element_type=F32)
    queries = (projected[0] + qv_bias[0]).astype(BF16).reshape(head_shape)
    keys_low = projected[1].astype(BF16).reshape(head_shape)
    values_low = (projected[2] + qv_bias[1]).astype(BF16).reshape(head_shape)
    scores = (
        jnp.einsum("lqhd,lkhd->lhqk", queries, keys_low, preferred_element_type=F32) * score_scale
    )
    top_score = jnp.max(scores, -1, keepdims=True)
    exponent = jnp.exp(scores - top_score)
    exp_sums = jnp.sum(exponent, -1, keepdims=True)
    probs = exponent / exp_sums
    probs_low = probs.astype(BF16)
    attended = jnp.einsum("lhqk,lkhd->lqhd", probs_low, values_low, preferred_element_type=F32)
    attended = attended.astype(BF16).reshape(rows, width)
    attn_term = jnp.einsum("rc,oc->ro", attended, proj_full, preferred_element_type=F32)
    attn_out, middle, normed_two, inverse_two, full_two = call(
        middle_kernel,
        2,
        [own_f32, own_f32, own_f32, one_f32, full_low],
        scatter_bufs + [buf, stats],
        9,
        attn_term.astype(BF16),
        field_in,
        mod,
        proj_bias[None],
    )
    pre_act = jnp.dot(full_two, fc1_full, preferred_element_type=F32) + fc1_bias
    act_value, gelu_back = jax.vjp(partial(jax.nn.gelu, approximate=True), pre_act)
    act_low = act_value.astype(BF16)
    grad_act = jnp.dot(grad_mlp_full, fc2_full, preferred_element_type=F32)
    grad_pre = gelu_back(grad_act)[0].astype(BF16)
    mlp_term = jnp.einsum("rf,of->ro", act_low, fc2_full, preferred_element_type=F32)
    hidden_two_term = jnp.einsum("rf,kf->rk", grad_pre, fc1_full, preferred_element_type=F32)
    grad_middle, grad_attn_full, output, two_sums, proj_bias_grad = call(
        back_kernel,
        3,
        [own_f32, full_low, own_f32, ((lat * 4, width), F32), line],
        scatter_bufs + scatter_bufs + [buf, stats],
        12,
        hidden_two_term.astype(BF16),
        mlp_term.astype(BF16),
        grad_out,
        normed_two,
        inverse_two,
        mod,
        fc2_bias[None],
        middle,
        attn_out,
    )
    fc2_grad = jnp.einsum("ro,rf->of", grad_mlp_full, act_low, preferred_element_type=F32)
    fc2_shard = scatter_rows(fc2_grad.astype(BF16), 0, tok_count, down[::-1])
    fc1_bias_grad = jnp.sum(grad_pre, 0, dtype=F32)
    fc1_grad = jnp.einsum("rk,rf->kf", full_two, grad_pre, preferred_element_type=F32)
    fc1_shard = scatter_rows(fc1_grad.astype(BF16), 0, tok_count, mixed[::-1])
    proj_grad = jnp.einsum("ro,rc->oc", grad_attn_full, attended, preferred_element_type=F32)
    proj_shard = scatter_rows(proj_grad.astype(BF16), 0, tok_count, mixed[::-1])
    grad_attended = (
        jnp.dot(grad_attn_full, proj_full, preferred_element_type=F32)
        .astype(BF16)
        .reshape(head_shape)
    )
    grad_values = jnp.einsum(
        "lhqk,lqhd->lkhd", probs_low, grad_attended, preferred_element_type=F32
    )
    grad_probs = jnp.einsum(
        "lqhd,lkhd->lhqk", grad_attended, values_low, preferred_element_type=F32
    )
    grad_scores = (
        probs * (grad_probs - jnp.sum(grad_probs * probs, -1, keepdims=True))
    ).astype(BF16)
    grad_queries = (
        jnp.einsum("lhqk,lkhd->lqhd", grad_scores, keys_low, preferred_element_type=F32)
        * score_scale
    )
    grad_keys = (
        jnp.einsum("lhqk,lqhd->lkhd", grad_scores, queries, preferred_element_type=F32)
        * score_scale
    )
    grad_qkv = (
        jnp.stack([grad_queries, grad_keys, grad_values]).astype(BF16).reshape(3, rows, width)
    )
    hidden_one_term = jnp.einsum("jrc,jkc->rk", grad_qkv, qkv_full, preferred_element_type=F32)
    tokens_grad, one_sums = call(
        close_kernel,
        4,
        [own_f32, ((lat * 2, width), F32)],
        scatter_bufs + [stats],
        6,
        hidden_one_term.astype(BF16),
        normed_one,
        inverse_one,
        mod,
        grad_middle,
    )
    qkv_grad = jnp.einsum("rk,jrc->jkc", full_one, grad_qkv, preferred_element_type=F32)
    qkv_shard = scatter_rows(qkv_grad.astype(BF16), 1, tok_count, down[::-1])
    qv_bias_grad = jnp.stack([jnp.sum(grad_qkv[0], 0, dtype=F32), jnp.sum(grad_qkv[2], 0, dtype=F32)])

    ones = one_sums.reshape(lat, 2, width)
    twos = two_sums.reshape(lat, 4, width)
    grad_mod = jnp.stack(
        [ones[:, 0], ones[:, 1], twos[:, 2], twos[:, 0], twos[:, 1], twos[:, 3]], 1
    ).astype(BF16)
    bias_terms = jnp.concatenate(
        [qv_bias_grad.reshape(-1), proj_bias_grad[0], fc1_bias_grad, fc2_bias_grad[0]]
    )
    bias_sums = lax.psum(bias_terms, "tok")
    grad_mod_all = lax.all_gather(grad_mod, "tok", axis=0, tiled=True)
    ada_bias_sum = jnp.sum(grad_mod_all, 0, dtype=F32)
    ada_shard = jnp.einsum("lk,ljc->jkc", cond_rows, grad_mod_all, preferred_element_type=F32)
    cond_term = jnp.einsum("ljc,jkc->lk", grad_mod_all, ada_weight, preferred_element_type=F32)
    cond_terms = lax.all_gather(cond_term, ("tok", "feat"), axis=0, tiled=False)
    grad_cond_act = (
        jnp.sum(cond_terms.reshape(tok_count, FEAT, tok_count * lat, part), 1)
        .transpose(1, 0, 2)
        .reshape(tok_count * lat, D)
    )
    own_cond = lax.dynamic_slice_in_dim(cond_all, offset, width, 1)
    own_grad = lax.dynamic_slice_in_dim(grad_cond_act, offset, width, 1)
    grad_condition = jax.vjp(jax.nn.silu, own_cond)[1](own_grad)[0]
    class_count = class_table.shape[1]
    one_hot = (
        labels_all[:, None] == jnp.arange(class_count, dtype=jnp.int32)[None, :]
    ).astype(F32)
    class_sum = jnp.einsum("lc,lw->wc", one_hot, grad_condition, precision=lax.Precision.HIGHEST)
    inner = fc1_bias.shape[0]
    return (
        output.T,
        tokens_grad.T,
        class_sum,
        ada_shard,
        ada_bias_sum,
        qkv_shard,
        bias_sums[: 2 * width].reshape(2, width),
        proj_shard,
        bias_sums[2 * width : 3 * width],
        fc1_shard,
        bias_sums[3 * width : 3 * width + inner],
        fc2_shard,
        bias_sums[3 * width + inner :],
    )


def solution(mesh):
    return jax.shard_map(
        partial(per_device, mesh.shape["tok"]),
        mesh=mesh,
        in_specs=(
            P("feat", "tok"),
            P("tok"),
            P("tok"),
            P("feat", None),
            P(None, "tok", "feat"),
            P(None, "feat"),
            P(None, "tok", "feat"),
            P(None, "feat"),
            P("tok", "feat"),
            P("feat"),
            P("tok", "feat"),
            P("feat"),
            P("tok", "feat"),
            P("feat"),
            P("feat", "tok"),
        ),
        out_specs=(
            P("feat", "tok"),
            P("feat", "tok"),
            P("feat", None),
            P(None, "tok", "feat"),
            P(None, "feat"),
            P(None, "tok", "feat"),
            P(None, "feat"),
            P("tok", "feat"),
            P("feat"),
            P("tok", "feat"),
            P("feat"),
            P("tok", "feat"),
            P("feat"),
        ),
        check_vma=False,
    )
```

time: 822 us -> 440 us (0.54)
  waiting for transfers between devices: 468 us -> 53.3 us
  Pallas kernels: 0 us -> 92.8 us
  blocking collectives: 193 us -> 139 us
  starting transfers between devices: 0.79 us -> 25.9 us
  local copies, waits for them, and re-layouts: 77.9 us -> 58.5 us
  between operations: 14.6 us -> 2.89 us
  matrix products: 40.2 us -> 28.7 us
    reduce_scatter x7 -> x0, waiting for transfers between devices: 272 us -> none  [the longest x1 72.6 us: per_device(): lax.psum_scatter(fc1_grad, 'tok', scatter_dimension=0, tiled=True)]
    unnamed x17 -> x0, waiting for transfers between devices: 102 us -> none
    pallas_call x0 -> x5, Pallas kernels: none -> 92.8 us  [call(): pl.pallas_call(kernel, out_shape=out_shape, in_specs=[VMEM] * len(args),...]
    psum x1 -> x0, waiting for transfers between devices: 77.5 us -> none  [per_device(): lax.psum((class_grad, ada_bias_grad, qv_bias_grad, proj_bias_grad, fc1_bi...]
    ppermute x0 -> x24, waiting for transfers between devices: none -> 53.3 us  [the longest x12 35.8 us: scatter_rows(): got = lax.ppermute(sent, 'tok', [(i, i ^ bit) for i in range(count)])]
    psum x7 -> x1, blocking collectives: 75.3 us -> 23.4 us  [per_device(): bias_sums = lax.psum(bias_terms, 'tok')]
    ppermute x0 -> x24, starting transfers between devices: none -> 25.9 us  [the longest x12 15.8 us: gather_rows(): other = lax.ppermute(held, 'tok', [(i, i ^ bit) for i in range(count)])]
    unnamed x163 -> x122, local copies, waits for them, and re-layouts: 43.6 us -> 18.4 us
  transfers between devices with their start and end apart: 14 -> 24, of which waited for: 11 -> 11; matrix products, arithmetic and copies ran while one was open for 10% -> 17% of each run, Pallas kernels for 0% -> 12%
where the time goes in v1:
time: 440 us; the launch traced here: 432 us
  blocking collectives  139 us (32%)
  Pallas kernels  92.8 us (21%)
  local copies, waits for them, and re-layouts  58.5 us (13%)
  waiting for transfers between devices  53.3 us (12%)
  other arithmetic  30.4 us (7%)
  matrix products  28.7 us (7%)
  starting transfers between devices  25.9 us (6%)
    pallas_call x5, Pallas kernels, call(): pl.pallas_call(kernel, out_shape=out_shape, in_specs=[VMEM] * len(args),...  92.8 us
    all_gather x1, blocking collectives, per_device(): cond_all = lax.all_gather(condition, ('tok', 'feat'), axis=0, tiled=False)  42.4 us
    all_gather x1, blocking collectives, per_device(): cond_terms = lax.all_gather(cond_term, ('tok', 'feat'), axis=0, tiled=False)  37.3 us
    ppermute x12, waiting for transfers between devices, scatter_rows(): got = lax.ppermute(sent, 'tok', [(i, i ^ bit) for i in range(count)])  35.8 us
    all_gather x1, blocking collectives, per_device(): grad_mod_all = lax.all_gather(grad_mod, 'tok', axis=0, tiled=True)  30.5 us
    psum x1, blocking collectives, per_device(): bias_sums = lax.psum(bias_terms, 'tok')  23.4 us
    unnamed x122, local copies, waits for them, and re-layouts  18.4 us
    ppermute x12, waiting for transfers between devices, gather_rows(): other = lax.ppermute(held, 'tok', [(i, i ^ bit) for i in range(count)])  17.5 us
  transfers between devices with their start and end apart: 24, of which 11 were waited for; matrix products, arithmetic and copies ran while one was open for 17% of the time, Pallas kernels for 12%

profile of v1, /device:TPU:0, one launch (start us, length us, event | category | flops | bytes accessed | tf_op | source)
XLA Modules:
  0.0 431.6 jit_solution(2265974621121754515)
XLA Ops:
  0.7 3.0 collective-permute-start.6
  3.7 2.6 collective-permute-start.3
  10.9 42.4 %all-gather.2 = f32[32,2,192]{2,1,0:T(2,128)S(1)} all-gather(f32[1,2,192]{2,1,0:T(2,128)S(1)} %fusion.61), channel_id=2, replica_groups=mesh['tok'=8,'feat'=4] {'tok','feat'}, dimensions={0}, use_global_device_ids=true | all-gather | bytes 50688 | tf_op jit(solution)/shard_map/all_gather | solution.py:396
  55.1 5.6 %all-reduce = s32[16]{0:T(128)S(1)} all-reduce(s32[16]{0:T(128)S(1)} %dynamic-update-slice), channel_id=1, replica_groups=mesh['tok'=8,'feat'=4] {'tok'}, use_global_device_ids=true, to_apply=%add | all-reduce | flops 16 | bytes 128
  60.8 3.3 collective-permute-start.7
  64.8 9.2 %shard_map.246.mod = f32[12,192]{1,0:T(8,128)S(1)} custom-call(f32[8,12,192]{2,1,0:T(8,128)S(1)} %reshape.213.term, f32[12,192]{1,0:T(8,128)S(1)} %tile.10.bias), custom_call_target="tpu_custom_call" | custom-call | tf_op jit(solution)/shard_map/pallas_call | solution.py:305
  74.0 18.4 %shard_map.247 = (bf16[512,768]{1,0:T(8,128)(2,1)S(1)}, bf16[512,768]{1,0:T(8,128)(2,1)S(1)}, f32[512,192]{1,0:T(8,128)S(1)}, f32[512,1]{1,0:T(8,128)S(1)}, f32[1,192]{1,0:T(1,128)S(1)}) custom-call(f32[512,192]{1,0:T(8,128)S(1)} %bitcast.220, f32[12,192]{1,0:T(8,128)S(1)} %shard_map.246.mod, f32[512,192]{1,0:T(8,128)S(1)} %bitcast.218), custom_call_target="tpu_custom_call" | custom-call | tf_op jit(solution)/shard_map/pallas_call | solution.py:305
  105.3 6.7 %collective-permute-done.4 = bf16[3,2,96,192]{3,2,0,1:T(8,128)(2,1)} collective-permute-done((bf16[3,2,96,192]{3,2,0,1:T(8,128)(2,1)}, bf16[3,2,96,192]{3,2,0,1:T(8,128)(2,1)}, u32[]{:S(2)}, u32[]{:S(2)}) %collective-permute-start.4) | collective-permute-done | bytes 221216 | tf_op jit(solution)/shard_map/ppermute | solution.py:334
  116.6 2.8 collective-permute-done.1
  122.2 7.4 %collective-permute-done.5 = bf16[3,2,2,96,192]{4,3,0,1,2:T(8,128)(2,1)S(1)} collective-permute-done((bf16[3,2,2,96,192]{4,3,0,1,2:T(8,128)(2,1)S(1)}, bf16[3,2,2,96,192]{4,3,0,1,2:T(8,128)(2,1)S(1)}, u32[]{:S(2)}, u32[]{:S(2)}) %collective-permute-start.5) | collective-permute-done | bytes 442400 | tf_op jit(solution)/shard_map/ppermute | solution.py:334
  131.0 3.8 copy.142
  134.8 5.0 %reshape.215 = bf16[3,768,192]{1,2,0:T(8,128)(2,1)} reshape(bf16[3,2,2,2,96,192]{4,3,2,1,5,0:T(2,128)(2,1)} %copy.142) | data formatting | bytes 1769472 | tf_op jit(solution)/shard_map/reshape | solution.py:343
  139.8 1.8 convolution_bitcast_fusion
  142.6 2.1 squeeze.9
  144.7 2.9 fusion.75
  147.6 2.0 squeeze.8
  149.6 1.8 fusion.13
  152.2 23.0 %shard_map.248 = (f32[512,192]{1,0:T(8,128)S(1)}, f32[512,192]{1,0:T(8,128)S(1)}, f32[512,192]{1,0:T(8,128)S(1)}, f32[512,1]{1,0:T(8,128)S(1)}, bf16[512,768]{1,0:T(8,128)(2,1)S(1)}) custom-call(bf16[512,768]{1,0:T(8,128)(2,1)S(1)} %convolution_convert_fusion.5.term, f32[512,192]{1,0:T(8,128)S(1)} %bitcast.221, f32[12,192]{1,0:T(8,128)S(1)} %shard_map.246.mod, ...), custom_call_target="tpu_custom_call" | custom-call | tf_op jit(solution)/shard_map/pallas_call | solution.py:305
  183.0 2.0 convolution_convert_fusion
  185.8 27.6 %shard_map.249 = (f32[512,192]{1,0:T(8,128)S(1)}, bf16[512,768]{1,0:T(8,128)(2,1)S(1)}, f32[512,192]{1,0:T(8,128)S(1)}, f32[8,192]{1,0:T(8,128)S(1)}, f32[1,192]{1,0:T(1,128)S(1)}) custom-call(bf16[512,768]{1,0:T(8,128)(2,1)S(1)} %convolution_convert_fusion.4.term, bf16[512,768]{1,0:T(8,128)(2,1)S(1)} %convolution_convert_fusion.3.mlp_term, ...), custom_call_target="tpu_custom_call" | custom-call | tf_op jit(solution)/shard_map/pallas_call | solution.py:305
  215.7 2.0 convolution_convert_fusion.6
  217.7 1.8 convolution_convert_fusion.1
  219.6 2.2 convert_reduce_fusion.1
  226.7 1.8 copy.155
  228.5 1.7 stack.179
  234.0 1.6 fusion.10
  235.6 14.6 %shard_map.250 = (f32[512,192]{1,0:T(8,128)S(1)}, f32[4,192]{1,0:T(4,128)S(1)}) custom-call(bf16[512,768]{1,0:T(8,128)(2,1)S(1)} %bitcast_convert_fusion.term, f32[512,192]{1,0:T(8,128)S(1)} %get-tuple-element.39.normed_in, f32[512,1]{1,0:T(8,128)S(1)} %copy-done.4, f32[12,192]{1,0:T(8,128)S(1)} %shard_map.246.mod, f32[512,192]{1,0:T(8,128)S(1)} %copy-done.2), custom_call_target="tpu_custom_call" | custom-call | tf_op jit(solution)/shard_map/pallas_call | solution.py:305
  250.3 30.5 %all_gather.20 = bf16[16,6,192]{2,1,0:T(8,128)(2,1)S(1)} all-gather(bf16[2,6,192]{2,1,0:T(8,128)(2,1)S(1)} %pad_maximum_fusion.12), channel_id=1, replica_groups=mesh['tok'=8,'feat'=4] {'tok'}, dimensions={0}, use_global_device_ids=true | all-gather | bytes 41472 | tf_op jit(solution)/shard_map/all_gather | solution.py:551
  283.2 2.3 reshape.227
  285.4 2.0 fusion.72
  288.5 1.8 copy.179
  292.9 2.0 collective-permute-start.18
  295.1 23.4 %psum.7 = f32[1536]{0:T(1024)S(1)} all-reduce(f32[1536]{0:T(1024)S(1)} %concatenate.9), channel_id=1, replica_groups=mesh['tok'=8,'feat'=4] {'tok'}, use_global_device_ids=true, to_apply=%region_8.9 | all-reduce | flops 1536 | bytes 12288 | tf_op jit(solution)/shard_map/psum | solution.py:550
  319.2 37.3 %all-gather.1 = f32[512,96]{1,0:T(8,128)S(1)} all-gather(f32[16,96]{1,0:T(8,128)S(1)} %convolution_bitcast_fusion.2), channel_id=3, replica_groups=mesh['tok'=8,'feat'=4] {'tok','feat'}, dimensions={0}, use_global_device_ids=true | all-gather | bytes 202752 | tf_op jit(solution)/shard_map/all_gather | solution.py:555
  357.3 4.6 %reshape.224 = bf16[3,2,2,2,96,192]{4,3,2,1,5,0:T(2,128)(2,1)S(1)} reshape(bf16[3,768,192]{1,2,0:T(8,128)(2,1)} %fusion.10) | data formatting | bytes 1769472 | tf_op jit(solution)/shard_map/reshape | solution.py:351
  361.9 3.1 fusion.70
  365.0 2.4 copy.178
  367.5 2.4 copy.177
  373.2 5.3 %collective-permute-done.16 = bf16[2,96,192]{2,1,0:T(8,128)(2,1)S(1)} collective-permute-done((bf16[2,96,192]{2,1,0:T(8,128)(2,1)S(1)}, bf16[2,96,192]{2,1,0:T(8,128)(2,1)S(1)}, u32[]{:S(2)}, u32[]{:S(2)}) %collective-permute-start.16) | collective-permute-done | bytes 73760 | tf_op jit(solution)/shard_map/ppermute | solution.py:357
  378.5 1.8 collective-permute-start.17
  380.3 2.2 fusion.37
  384.2 2.1 copy.172
  392.0 2.0 collective-permute-start.22
  395.3 5.3 %collective-permute-done.13 = bf16[3,2,96,192]{3,2,0,1:T(8,128)(2,1)S(1)} collective-permute-done((bf16[3,2,96,192]{3,2,0,1:T(8,128)(2,1)S(1)}, bf16[3,2,96,192]{3,2,0,1:T(8,128)(2,1)S(1)}, u32[]{:S(2)}, u32[]{:S(2)}) %collective-permute-start.13) | collective-permute-done | bytes 221216 | tf_op jit(solution)/shard_map/ppermute | solution.py:357
  400.8 3.0 collective-permute-start.19
  403.8 13.9 %collective-permute-done.14 = bf16[3,96,192]{2,1,0:T(8,128)(2,1)S(1)} collective-permute-done((bf16[3,96,192]{2,1,0:T(8,128)(2,1)S(1)}, bf16[3,96,192]{2,1,0:T(8,128)(2,1)S(1)}, u32[]{:S(2)}, u32[]{:S(2)}) %collective-permute-start.14) | collective-permute-done | bytes 110624 | tf_op jit(solution)/shard_map/ppermute | solution.py:357
  418.7 6.4 %collective-permute-done.19 = bf16[2,96,768]{2,1,0:T(8,128)(2,1)S(1)} collective-permute-done((bf16[2,96,768]{2,1,0:T(8,128)(2,1)S(1)}, bf16[2,96,768]{2,1,0:T(8,128)(2,1)S(1)}, u32[]{:S(2)}, u32[]{:S(2)}) %collective-permute-start.19) | collective-permute-done | bytes 294944 | tf_op jit(solution)/shard_map/ppermute | solution.py:357
  427.4 3.0 collective-permute-done.20
  (264 shorter events, 72.8 us)
Async XLA Ops:
  0.6 54.2 %copy-start = (bf16[6,96,192]{2,1,0:T(8,128)(2,1)S(1)}, bf16[6,96,192]{2,1,0:T(8,128)(2,1)}, u32[]{:S(2)}) copy-start(bf16[6,96,192]{2,1,0:T(8,128)(2,1)} %param.19) | copy-start | bytes 663556
  0.7 52.7 %copy-start.50 = (u32[32]{0:T(128)S(1)}, u32[32]{0:T(128)}, u32[]{:S(2)}) copy-start(u32[32]{0:T(128)} %constant.198) | copy-start | bytes 388
  0.7 60.1 %copy-start.44 = (bf16[96,192]{1,0:T(8,128)(2,1)S(1)}, bf16[96,192]{1,0:T(8,128)(2,1)}, u32[]{:S(2)}) copy-start(bf16[96,192]{1,0:T(8,128)(2,1)} %param.23) | copy-start | bytes 110596
  0.7 53.9 %copy-start.49 = (s32[2]{0:T(128)S(1)}, s32[2]{0:T(128)}, u32[]{:S(2)}) copy-start(s32[2]{0:T(128)} %param.17) | copy-start | bytes 28
  0.7 63.4 %copy-start.47 = (f32[2,192]{1,0:T(2,128)S(1)}, f32[2,192]{1,0:T(2,128)}, u32[]{:S(2)}) copy-start(f32[2,192]{1,0:T(2,128)} %param.22) | copy-start | bytes 4612
  0.7 63.5 %copy-start.46 = (f32[6,192]{1,0:T(8,128)S(1)}, f32[6,192]{1,0:T(8,128)}, u32[]{:S(2)}) copy-start(f32[6,192]{1,0:T(8,128)} %param.20) | copy-start | bytes 13828
  0.7 60.0 %collective-permute-start.6 = (bf16[96,192]{1,0:T(8,128)(2,1)}, bf16[96,192]{1,0:T(8,128)(2,1)S(1)}, u32[]{:S(2)}, u32[]{:S(2)}) collective-permute-start(bf16[96,192]{1,0:T(8,128)(2,1)} %param.23), channel_id=1, source_target_pairs={{0,4},{4,0},{8,12},{12,8},{16,20},{20,16},{24,28},{28,24},{1,5},{5... | collective-permute-start | bytes 110600 | tf_op jit(solution)/shard_map/ppermute | solution.py:334
  3.7 89.8 %collective-permute-start.3 = (bf16[3,96,192]{2,1,0:T(8,128)(2,1)}, bf16[3,96,192]{2,1,0:T(8,128)(2,1)}, u32[]{:S(2)}, u32[]{:S(2)}) collective-permute-start(bf16[3,96,192]{2,1,0:T(8,128)(2,1)} %param.21), channel_id=1, source_target_pairs={{0,16},{4,20},{8,24},{12,28},{16,0},{20,4},{24,8},{28,12},{1,17},{... | collective-permute-start | bytes 331784 | tf_op jit(solution)/shard_map/ppermute | solution.py:334
  6.3 90.1 %collective-permute-start.9 = (bf16[96,768]{1,0:T(8,128)(2,1)}, bf16[96,768]{1,0:T(8,128)(2,1)}, u32[]{:S(2)}, u32[]{:S(2)}) collective-permute-start(bf16[96,768]{1,0:T(8,128)(2,1)} %param.25), channel_id=1, source_target_pairs={{0,4},{4,0},{8,12},{12,8},{16,20},{20,16},{24,28},{28,24},{1,5},{5... | collective-permute-start | bytes 442376 | tf_op jit(solution)/shard_map/ppermute | solution.py:334
  6.8 92.6 %collective-permute-start = (bf16[96,768]{1,0:T(8,128)(2,1)}, bf16[96,768]{1,0:T(8,128)(2,1)}, u32[]{:S(2)}, u32[]{:S(2)}) collective-permute-start(bf16[96,768]{1,0:T(8,128)(2,1)} %param.27), channel_id=1, source_target_pairs={{0,16},{4,20},{8,24},{12,28},{16,0},{20,4},{24,8},{28,12},{1,17},{... | collective-permute-start | bytes 442376 | tf_op jit(solution)/shard_map/ppermute | solution.py:334
  8.8 55.5 %copy-start.38 = (f32[192,512]{1,0:T(8,128)S(1)}, f32[192,512]{1,0:T(8,128)}, u32[]{:S(2)}) copy-start(f32[192,512]{1,0:T(8,128)} %param.15) | copy-start | bytes 1179652
  10.2 54.3 %copy-start.39 = (f32[192,512]{1,0:T(8,128)S(1)}, f32[192,512]{1,0:T(8,128)}, u32[]{:S(2)}) copy-start(f32[192,512]{1,0:T(8,128)} %param.29) | copy-start | bytes 1179652
  60.8 31.7 %collective-permute-start.7 = (bf16[2,96,192]{2,1,0:T(8,128)(2,1)S(1)}, bf16[2,96,192]{2,1,0:T(8,128)(2,1)S(1)}, u32[]{:S(2)}, u32[]{:S(2)}) collective-permute-start(bf16[2,96,192]{2,1,0:T(8,128)(2,1)S(1)} %pad_maximum_fusion.11), channel_id=1, source_target_pairs={{0,16},{4,20},{8,24},{12,28},{16,0},{20,4},{24,8},{28,12},{1,17},{... | collective-permute-start | bytes 221192 | tf_op jit(solution)/shard_map/ppermute | solution.py:334
  64.8 28.8 %copy-start.41 = (bf16[3,96,192]{2,1,0:T(8,128)(2,1)S(1)}, bf16[3,96,192]{2,1,0:T(8,128)(2,1)}, u32[]{:S(2)}) copy-start(bf16[3,96,192]{2,1,0:T(8,128)(2,1)} %param.21) | copy-start | bytes 331780
  64.8 31.7 %copy-start.42 = (bf16[96,768]{1,0:T(8,128)(2,1)S(1)}, bf16[96,768]{1,0:T(8,128)(2,1)}, u32[]{:S(2)}) copy-start(bf16[96,768]{1,0:T(8,128)(2,1)} %param.25) | copy-start | bytes 442372
  92.5 7.0 %copy-start.43 = (bf16[96,768]{1,0:T(8,128)(2,1)S(1)}, bf16[96,768]{1,0:T(8,128)(2,1)}, u32[]{:S(2)}) copy-start(bf16[96,768]{1,0:T(8,128)(2,1)} %param.27) | copy-start | bytes 442372
  92.6 10.1 %collective-permute-start.8 = (bf16[2,2,96,192]{3,2,1,0:T(8,128)(2,1)S(1)}, bf16[2,2,96,192]{3,2,1,0:T(8,128)(2,1)S(1)}, u32[]{:S(2)}, u32[]{:S(2)}) collective-permute-start(bf16[2,2,96,192]{3,2,1,0:T(8,128)(2,1)S(1)} %pad_maximum_fusion.10), channel_id=1, source_target_pairs={{0,8},{4,12},{8,0},{12,4},{16,24},{20,28},{24,16},{28,20},{1,9},{5... | collective-permute-start | bytes 442376 | tf_op jit(solution)/shard_map/ppermute | solution.py:334
  95.3 16.6 %collective-permute-start.4 = (bf16[3,2,96,192]{3,2,0,1:T(8,128)(2,1)}, bf16[3,2,96,192]{3,2,0,1:T(8,128)(2,1)}, u32[]{:S(2)}, u32[]{:S(2)}) collective-permute-start(bf16[3,2,96,192]{3,2,0,1:T(8,128)(2,1)} %pad_maximum_fusion.8), channel_id=1, source_target_pairs={{0,8},{4,12},{8,0},{12,4},{16,24},{20,28},{24,16},{28,20},{1,9},{5... | collective-permute-start | bytes 663560 | tf_op jit(solution)/shard_map/ppermute | solution.py:334
  98.2 16.4 %collective-permute-start.10 = (bf16[2,96,768]{2,1,0:T(8,128)(2,1)}, bf16[2,96,768]{2,1,0:T(8,128)(2,1)}, u32[]{:S(2)}, u32[]{:S(2)}) collective-permute-start(bf16[2,96,768]{2,1,0:T(8,128)(2,1)} %pad_maximum_fusion.9), channel_id=1, source_target_pairs={{0,16},{4,20},{8,24},{12,28},{16,0},{20,4},{24,8},{28,12},{1,17},{... | collective-permute-start | bytes 884744 | tf_op jit(solution)/shard_map/ppermute | solution.py:334
  101.2 18.3 %collective-permute-start.1 = (bf16[2,96,768]{2,1,0:T(8,128)(2,1)}, bf16[2,96,768]{2,1,0:T(8,128)(2,1)}, u32[]{:S(2)}, u32[]{:S(2)}) collective-permute-start(bf16[2,96,768]{2,1,0:T(8,128)(2,1)} %pad_maximum_fusion.7), channel_id=1, source_target_pairs={{0,8},{4,12},{8,0},{12,4},{16,24},{20,28},{24,16},{28,20},{1,9},{5... | collective-permute-start | bytes 884744 | tf_op jit(solution)/shard_map/ppermute | solution.py:334
  105.2 46.5 %copy-start.14 = (bf16[768,192]{0,1:T(8,128)(2,1)}, bf16[768,192]{0,1:T(8,128)(2,1)S(1)}, u32[]{:S(2)}) copy-start(bf16[768,192]{0,1:T(8,128)(2,1)S(1)} %reshape.217) | copy-start | bytes 884740
  105.2 9.4 %copy-start.30 = (bf16[1,96,768]{2,1,0:T(8,128)(2,1)S(1)}, bf16[1,96,768]{2,1,0:T(8,128)(2,1)}, u32[]{:S(2)}) copy-start(bf16[1,96,768]{2,1,0:T(8,128)(2,1)} %copy-done.29) | copy-start | bytes 442372
  105.3 9.4 %copy-start.32 = (bf16[1,96,768]{2,1,0:T(8,128)(2,1)S(1)}, bf16[1,96,768]{2,1,0:T(8,128)(2,1)}, u32[]{:S(2)}) copy-start(bf16[1,96,768]{2,1,0:T(8,128)(2,1)} %copy-done.31) | copy-start | bytes 442372
  113.1 6.3 %copy-start.28 = (bf16[1,96,768]{2,1,0:T(8,128)(2,1)S(1)}, bf16[1,96,768]{2,1,0:T(8,128)(2,1)}, u32[]{:S(2)}) copy-start(bf16[1,96,768]{2,1,0:T(8,128)(2,1)} %copy-done.27) | copy-start | bytes 442372
  113.2 16.3 %collective-permute-start.5 = (bf16[3,2,2,96,192]{4,3,0,1,2:T(8,128)(2,1)S(1)}, bf16[3,2,2,96,192]{4,3,0,1,2:T(8,128)(2,1)S(1)}, u32[]{:S(2)}, u32[]{:S(2)}) collective-permute-start(bf16[3,2,2,96,192]{4,3,0,1,2:T(8,128)(2,1)S(1)} %pad_maximum_fusion.4), channel_id=1, source_target_pairs={{0,4},{4,0},{8,12},{12,8},{16,20},{20,16},{24,28},{28,24},{1,5},{5... | collective-permute-start | bytes 1327112 | tf_op jit(solution)/shard_map/ppermute | solution.py:334
  115.6 5.8 %copy-start.15 = (bf16[1,2,96,768]{3,2,1,0:T(8,128)(2,1)}, bf16[1,2,96,768]{3,2,1,0:T(8,128)(2,1)S(1)}, u32[]{:S(2)}) copy-start(bf16[1,2,96,768]{3,2,1,0:T(8,128)(2,1)S(1)} %get-tuple-element.117) | copy-start | bytes 884740
  115.6 5.8 %copy-start.17 = (bf16[1,2,96,768]{3,2,1,0:T(8,128)(2,1)}, bf16[1,2,96,768]{3,2,1,0:T(8,128)(2,1)S(1)}, u32[]{:S(2)}) copy-start(bf16[1,2,96,768]{3,2,1,0:T(8,128)(2,1)S(1)} %get-tuple-element.118) | copy-start | bytes 884740
  116.6 58.5 %collective-permute-start.11 = (bf16[2,2,96,768]{3,2,1,0:T(8,128)(2,1)}, bf16[2,2,96,768]{3,2,1,0:T(8,128)(2,1)}, u32[]{:S(2)}, u32[]{:S(2)}) collective-permute-start(bf16[2,2,96,768]{3,2,1,0:T(8,128)(2,1)} %pad_maximum_fusion.5), channel_id=1, source_target_pairs={{0,8},{4,12},{8,0},{12,4},{16,24},{20,28},{24,16},{28,20},{1,9},{5... | collective-permute-start | bytes 1769480 | tf_op jit(solution)/shard_map/ppermute | solution.py:334
  121.4 55.3 %collective-permute-start.2 = (bf16[2,2,96,768]{3,2,1,0:T(8,128)(2,1)}, bf16[2,2,96,768]{3,2,1,0:T(8,128)(2,1)}, u32[]{:S(2)}, u32[]{:S(2)}) collective-permute-start(bf16[2,2,96,768]{3,2,1,0:T(8,128)(2,1)} %pad_maximum_fusion.3), channel_id=1, source_target_pairs={{0,4},{4,0},{8,12},{12,8},{16,20},{20,16},{24,28},{28,24},{1,5},{5... | collective-permute-start | bytes 1769480 | tf_op jit(solution)/shard_map/ppermute | solution.py:334
  151.6 23.5 %copy-start.16 = (bf16[1,2,96,768]{3,2,1,0:T(8,128)(2,1)S(1)}, bf16[1,2,96,768]{3,2,1,0:T(8,128)(2,1)}, u32[]{:S(2)}) copy-start(bf16[1,2,96,768]{3,2,1,0:T(8,128)(2,1)} %copy-done.15) | copy-start | bytes 884740
  151.7 23.5 %copy-start.18 = (bf16[1,2,96,768]{3,2,1,0:T(8,128)(2,1)S(1)}, bf16[1,2,96,768]{3,2,1,0:T(8,128)(2,1)}, u32[]{:S(2)}) copy-start(bf16[1,2,96,768]{3,2,1,0:T(8,128)(2,1)} %copy-done.17) | copy-start | bytes 884740
  151.7 24.9 %copy-start.23 = (bf16[24,8,2,256]{3,1,2,0:T(8,128)(2,1)}, bf16[24,8,2,256]{3,1,2,0:T(8,128)(2,1)S(1)}, u32[]{:S(2)}) copy-start(bf16[24,8,2,256]{3,1,2,0:T(8,128)(2,1)S(1)} %copy.185) | copy-start | bytes 589828
  225.6 7.6 %copy-start.13 = (bf16[3,768,192]{1,2,0:T(8,128)(2,1)S(1)}, bf16[3,768,192]{1,2,0:T(8,128)(2,1)}, u32[]{:S(2)}) copy-start(bf16[3,768,192]{1,2,0:T(8,128)(2,1)} %reshape.215) | copy-start | bytes 2654212
  235.6 14.7 %slice-start = ((bf16[2,4,192]{2,1,0:T(4,128)(2,1)}), bf16[2,2,192]{2,1,0:T(2,128)(2,1)S(1)}, s32[]{:S(2)}) async-start(bf16[2,4,192]{2,1,0:T(4,128)(2,1)} %copy-done.45), calls=%async_computation | async-start | bytes 4096 | tf_op jit(solution)/shard_map/slice | solution.py:545
  235.6 47.4 %copy-start.35 = (bf16[768,768]{1,0:T(8,128)(2,1)S(1)}, bf16[768,768]{1,0:T(8,128)(2,1)}, u32[]{:S(2)}) copy-start(bf16[768,768]{1,0:T(8,128)(2,1)} %convolution_convert_fusion) | copy-start | bytes 3538948
  283.2 7.9 %copy-start.11 = (bf16[768,768]{1,0:T(8,128)(2,1)S(1)}, bf16[768,768]{1,0:T(8,128)(2,1)}, u32[]{:S(2)}) copy-start(bf16[768,768]{1,0:T(8,128)(2,1)} %convolution_convert_fusion.1) | copy-start | bytes 3538948
  291.1 80.4 %collective-permute-start.15 = (bf16[2,2,96,192]{3,2,1,0:T(8,128)(2,1)}, bf16[2,2,96,192]{3,2,1,0:T(8,128)(2,1)}, u32[]{:S(2)}, u32[]{:S(2)}) collective-permute-start(bf16[2,2,96,192]{3,2,1,0:T(8,128)(2,1)} %select_bitcast_fusion.15), channel_id=1, source_target_pairs={{0,8},{4,12},{8,0},{12,4},{16,24},{20,28},{24,16},{28,20},{1,9},{5... | collective-permute-start | bytes 442376 | tf_op jit(solution)/shard_map/ppermute | solution.py:357
  292.9 97.8 %collective-permute-start.21 = (bf16[2,2,96,768]{3,2,0,1:T(8,128)(2,1)}, bf16[2,2,96,768]{3,2,0,1:T(8,128)(2,1)}, u32[]{:S(2)}, u32[]{:S(2)}) collective-permute-start(bf16[2,2,96,768]{3,2,0,1:T(8,128)(2,1)} %select_bitcast_fusion), channel_id=1, source_target_pairs={{0,4},{4,0},{8,12},{12,8},{16,20},{20,16},{24,28},{28,24},{1,5},{5... | collective-permute-start | bytes 1769480 | tf_op jit(solution)/shard_map/ppermute | solution.py:357
  292.9 101.2 %collective-permute-start.18 = (bf16[2,2,96,768]{3,2,1,0:T(8,128)(2,1)}, bf16[2,2,96,768]{3,2,1,0:T(8,128)(2,1)}, u32[]{:S(2)}, u32[]{:S(2)}) collective-permute-start(bf16[2,2,96,768]{3,2,1,0:T(8,128)(2,1)} %select_bitcast_fusion.1), channel_id=1, source_target_pairs={{0,8},{4,12},{8,0},{12,4},{16,24},{20,28},{24,16},{28,20},{1,9},{5... | collective-permute-start | bytes 1769480 | tf_op jit(solution)/shard_map/ppermute | solution.py:357
  370.8 18.4 %collective-permute-start.12 = (bf16[3,2,2,96,192]{4,3,0,1,2:T(8,128)(2,1)}, bf16[3,2,2,96,192]{4,3,0,1,2:T(8,128)(2,1)}, u32[]{:S(2)}, u32[]{:S(2)}) collective-permute-start(bf16[3,2,2,96,192]{4,3,0,1,2:T(8,128)(2,1)} %select_bitcast_fusion.2), channel_id=1, source_target_pairs={{0,4},{4,0},{8,12},{12,8},{16,20},{20,16},{24,28},{28,24},{1,5},{5... | collective-permute-start | bytes 1327112 | tf_op jit(solution)/shard_map/ppermute | solution.py:357
  372.5 6.0 %collective-permute-start.16 = (bf16[2,96,192]{2,1,0:T(8,128)(2,1)S(1)}, bf16[2,96,192]{2,1,0:T(8,128)(2,1)S(1)}, u32[]{:S(2)}, u32[]{:S(2)}) collective-permute-start(bf16[2,96,192]{2,1,0:T(8,128)(2,1)S(1)} %fusion.36), channel_id=1, source_target_pairs={{0,16},{4,20},{8,24},{12,28},{16,0},{20,4},{24,8},{28,12},{1,17},{... | collective-permute-start | bytes 221192 | tf_op jit(solution)/shard_map/ppermute | solution.py:357
  378.5 9.2 %collective-permute-start.17 = (bf16[96,192]{1,0:T(8,128)(2,1)S(1)}, bf16[96,192]{1,0:T(8,128)(2,1)}, u32[]{:S(2)}, u32[]{:S(2)}) collective-permute-start(bf16[96,192]{1,0:T(8,128)(2,1)S(1)} %fusion.40), channel_id=1, source_target_pairs={{0,4},{4,0},{8,12},{12,8},{16,20},{20,16},{24,28},{28,24},{1,5},{5... | collective-permute-start | bytes 110600 | tf_op jit(solution)/shard_map/ppermute | solution.py:357
  390.5 10.0 %collective-permute-start.13 = (bf16[3,2,96,192]{3,2,0,1:T(8,128)(2,1)S(1)}, bf16[3,2,96,192]{3,2,0,1:T(8,128)(2,1)S(1)}, u32[]{:S(2)}, u32[]{:S(2)}) collective-permute-start(bf16[3,2,96,192]{3,2,0,1:T(8,128)(2,1)S(1)} %fusion.23), channel_id=1, source_target_pairs={{0,8},{4,12},{8,0},{12,4},{16,24},{20,28},{24,16},{28,20},{1,9},{5... | collective-permute-start | bytes 663560 | tf_op jit(solution)/shard_map/ppermute | solution.py:357
  392.0 26.4 %collective-permute-start.22 = (bf16[2,96,768]{2,1,0:T(8,128)(2,1)S(1)}, bf16[2,96,768]{2,1,0:T(8,128)(2,1)S(1)}, u32[]{:S(2)}, u32[]{:S(2)}) collective-permute-start(bf16[2,96,768]{2,1,0:T(8,128)(2,1)S(1)} %fusion.25), channel_id=1, source_target_pairs={{0,8},{4,12},{8,0},{12,4},{16,24},{20,28},{24,16},{28,20},{1,9},{5... | collective-permute-start | bytes 884744 | tf_op jit(solution)/shard_map/ppermute | solution.py:357
  400.7 17.0 %collective-permute-start.14 = (bf16[3,96,192]{2,1,0:T(8,128)(2,1)S(1)}, bf16[3,96,192]{2,1,0:T(8,128)(2,1)S(1)}, u32[]{:S(2)}, u32[]{:S(2)}) collective-permute-start(bf16[3,96,192]{2,1,0:T(8,128)(2,1)S(1)} %fusion.31), channel_id=1, source_target_pairs={{0,16},{4,20},{8,24},{12,28},{16,0},{20,4},{24,8},{28,12},{1,17},{... | collective-permute-start | bytes 331784 | tf_op jit(solution)/shard_map/ppermute | solution.py:357
  400.8 24.3 %collective-permute-start.19 = (bf16[2,96,768]{2,1,0:T(8,128)(2,1)S(1)}, bf16[2,96,768]{2,1,0:T(8,128)(2,1)S(1)}, u32[]{:S(2)}, u32[]{:S(2)}) collective-permute-start(bf16[2,96,768]{2,1,0:T(8,128)(2,1)S(1)} %fusion.24), channel_id=1, source_target_pairs={{0,16},{4,20},{8,24},{12,28},{16,0},{20,4},{24,8},{28,12},{1,17},{... | collective-permute-start | bytes 884744 | tf_op jit(solution)/shard_map/ppermute | solution.py:357
  418.6 8.1 %collective-permute-start.23 = (bf16[96,768]{1,0:T(8,128)(2,1)S(1)}, bf16[96,768]{1,0:T(8,128)(2,1)S(1)}, u32[]{:S(2)}, u32[]{:S(2)}) collective-permute-start(bf16[96,768]{1,0:T(8,128)(2,1)S(1)} %fusion.33), channel_id=1, source_target_pairs={{0,16},{4,20},{8,24},{12,28},{16,0},{20,4},{24,8},{28,12},{1,17},{... | collective-permute-start | bytes 442376 | tf_op jit(solution)/shard_map/ppermute | solution.py:357
  425.2 5.2 %collective-permute-start.20 = (bf16[96,768]{1,0:T(8,128)(2,1)S(1)}, bf16[96,768]{1,0:T(8,128)(2,1)S(1)}, u32[]{:S(2)}, u32[]{:S(2)}) collective-permute-start(bf16[96,768]{1,0:T(8,128)(2,1)S(1)} %fusion.32), channel_id=1, source_target_pairs={{0,4},{4,0},{8,12},{12,8},{16,20},{20,16},{24,28},{28,24},{1,5},{5... | collective-permute-start | bytes 442376 | tf_op jit(solution)/shard_map/ppermute | solution.py:357
  (30 other events, 73.5 us)

commit v2 on v1

--- a/solution.py
+++ b/solution.py
@@ -156,10 +156,10 @@
 
 
 def spread(mod, which, rows):
-    count = mod.shape[0] // 6
+    count = mod.shape[1]
     return jnp.concatenate(
         [
-            jnp.broadcast_to(mod[l * 6 + which : l * 6 + which + 1], (rows // count, mod.shape[1]))
+            jnp.broadcast_to(mod[which, l : l + 1], (rows // count, mod.shape[2]))
             for l in range(count)
         ],
         0,
@@ -174,26 +174,209 @@
         out[row : row + 1] = jnp.sum(values[l * seq : (l + 1) * seq], 0, keepdims=True)
 
 
-def open_kernel(x, mod, grad_out, full, grad_full, normed_out, inverse_out, fc2_sum, buf, grad_buf, stats, sems):
+def flip(t, *bits):
+    for bit in bits:
+        t = t + bit * (1 - 2 * ((t // bit) % 2))
+    return t
+
+
+def push_tok(src, dst, sems, at, peer):
+    return pltpu.make_async_remote_copy(
+        src_ref=src,
+        dst_ref=dst,
+        send_sem=sems.at[0, at],
+        recv_sem=sems.at[1, at],
+        device_id={"tok": peer},
+        device_id_type=MESH,
+    )
+
+
+def greet_all(count):
+    t = lax.axis_index("tok")
+    _, near, far, cross = partners()
+    barrier = pltpu.get_barrier_semaphore()
+    for peer in (near, far, cross):
+        pl.semaphore_signal(barrier, inc=1, device_id={"feat": peer}, device_id_type=MESH)
+    for step in range(1, count):
+        pl.semaphore_signal(
+            barrier, inc=1, device_id={"tok": (t + step) % count}, device_id_type=MESH
+        )
+    pl.semaphore_wait(barrier, FEAT - 1 + count - 1)
+
+
+def send_all(src, dst, sems, base, count):
+    t = lax.axis_index("tok")
+    copies = [
+        push_tok(src, dst, sems, base + step - 1, (t + step) % count) for step in range(1, count)
+    ]
+    for copy in copies:
+        copy.start()
+    return copies
+
+
+def wait_all(copies):
+    for copy in copies:
+        copy.wait()
+
+
+def block_at(ref, block, lead):
+    return ref.at[:, block] if lead else ref.at[block]
+
+
+class RowGather:
+    def __init__(self, block, full, lead, order, sems, base):
+        t = lax.axis_index("tok")
+        self.full, self.lead, self.order, self.sems, self.base = full, lead, list(order), sems, base
+        self.held, self.copies = [()], []
+        block_at(full, t, lead)[...] = block[...]
+        self.send()
+
+    def send(self):
+        t = lax.axis_index("tok")
+        bit = self.order[0]
+        self.copies = []
+        for held in self.held:
+            view = block_at(self.full, flip(t, *held), self.lead)
+            self.copies.append(push_tok(view, view, self.sems, self.base, flip(t, bit)))
+            self.base += 1
+        for copy in self.copies:
+            copy.start()
+
+    def step(self):
+        if not self.order:
+            return
+        wait_all(self.copies)
+        bit = self.order.pop(0)
+        self.held = self.held + [held + (bit,) for held in self.held]
+        if self.order:
+            self.send()
+
+
+class RowScatter:
+    def __init__(self, grad, out, acc, recv, lead, order, sems, base):
+        self.out, self.acc, self.recv, self.lead = out, acc, recv, lead
+        self.order, self.sems, self.base = list(order), sems, base
+        t = lax.axis_index("tok")
+        self.own = lambda held: block_at(grad, flip(t, *held), lead)
+        self.slot = 0
+        self.send()
+
+    def send(self):
+        t = lax.axis_index("tok")
+        bit, rest = self.order[0], self.order[1:]
+        self.kept = [()]
+        for other in rest:
+            self.kept = self.kept + [held + (other,) for held in self.kept]
+        self.copies = [
+            push_tok(
+                self.own((bit,) + held),
+                block_at(self.recv, self.slot + at, self.lead),
+                self.sems,
+                self.base + self.slot + at,
+                flip(t, bit),
+            )
+            for at, held in enumerate(self.kept)
+        ]
+        for copy in self.copies:
+            copy.start()
+
+    def step(self):
+        if not self.order:
+            return
+        places = {}
+        for at, held in enumerate(self.kept):
+            self.copies[at].wait()
+            slot = self.slot + at
+            total = self.own(held)[...].astype(F32) + block_at(self.recv, slot, self.lead)[
+                ...
+            ].astype(F32)
+            if len(self.order) == 1:
+                self.out[...] = total
+            else:
+                block_at(self.acc, slot, self.lead)[...] = total.astype(BF16)
+            places[frozenset(held)] = slot
+        self.slot += len(self.kept)
+        self.order.pop(0)
+        self.own = lambda held: block_at(self.acc, places[frozenset(held)], self.lead)
+        if self.order:
+            self.send()
+
+
+def head_kernel(
+    count, orders,
+    x, grad_out, cond, ada, bias, qkv, proj, fc1, fc2,
+    full, grad_full, normed_out, inverse_out, fc2_sum, mod, cond_all, cond_act, qkv_full, proj_full, fc1_full, fc2_full,
+    buf, grad_buf, stats, cond_rows, terms, got, sems, tok_sems,
+):
     f, near, far, cross = partners()
-    rows = x.shape[0]
+    t = lax.axis_index("tok")
+    rows, width = x.shape
+    lat = cond.shape[0]
+    part = ada.shape[1]
+    greet_all(count)
+    cond_all[t, f] = cond[...]
+    shares = [
+        push(cond_all.at[t, f], cond_all.at[t, f], sems, at, peer)
+        for at, peer in enumerate((near, far, cross))
+    ]
+    for copy in shares:
+        copy.start()
+    each = count - 1
+    weights = [RowGather(qkv, qkv_full, True, orders[0], tok_sems, 0)]
+    wait_all(shares)
+    sharing = send_all(cond_all.at[t], cond_all.at[t], tok_sems, 4 * each, count)
+    weights.append(RowGather(proj, proj_full, False, orders[1], tok_sems, each))
+    weights.append(RowGather(fc1, fc1_full, False, orders[1], tok_sems, 2 * each))
+    weights.append(RowGather(fc2, fc2_full, False, orders[0], tok_sems, 3 * each))
+    values = x[...]
+    mean, inverse = norm_stats(values, stats, sems, 3)
+    normed = (values - mean) * inverse
+    normed_out[...] = normed
+    inverse_out[...] = inverse
+    wait_all(sharing)
+    picked = jnp.zeros((count * lat, part), F32)
+    for block in range(FEAT):
+        for owner in range(count):
+            cond_rows[block, owner * lat : (owner + 1) * lat] = cond_all[owner, block]
+        value = cond_rows[block][:, :width]
+        act = (value / (1.0 + jnp.exp(-value))).astype(BF16)
+        chosen = (
+            lax.broadcasted_iota(jnp.int32, (width, part), 0) + block * width
+            == lax.broadcasted_iota(jnp.int32, (width, part), 1) + t * part
+        )
+        picked += jnp.dot(act, chosen.astype(F32).astype(BF16), preferred_element_type=F32)
+    picked = picked.astype(BF16)
+    cond_act[...] = picked
+    for which in range(6):
+        term = jnp.dot(picked, ada[which], preferred_element_type=F32)
+        for owner in range(count):
+            terms[owner, which] = term[owner * lat : (owner + 1) * lat]
+    copies = [
+        push_tok(terms.at[(t + step) % count], got.at[step - 1], tok_sems, 5 * each + step - 1, (t + step) % count)
+        for step in range(1, count)
+    ]
+    for copy in copies:
+        copy.start()
+    for weight in weights:
+        weight.step()
+    wait_all(copies)
+    mod[...] = terms[t] + jnp.sum(got[...], 0) + bias[...]
     mods = mod[...]
-    greet(near, far, cross)
+    buf[f] = (normed * (1.0 + spread(mods, 1, rows)) + spread(mods, 0, rows)).astype(BF16)
+    started = gather_start(buf, sems, 6)
     grad_mlp = (grad_out[...] * spread(mods, 5, rows)).astype(BF16)
     fc2_sum[...] = jnp.sum(grad_mlp.astype(F32), 0, keepdims=True)
     grad_buf[f] = grad_mlp
-    values = x[...]
-    mean, inverse = norm_stats(values, stats, sems, 0)
-    normed = (values - mean) * inverse
-    normed_out[...] = normed
-    inverse_out[...] = inverse
-    buf[f] = (normed * (1.0 + spread(mods, 1, rows)) + spread(mods, 0, rows)).astype(BF16)
-    started = gather_start(buf, sems, 3)
-    grad_started = gather_start(grad_buf, sems, 6)
-    relay = gather_forward(buf, sems, 3, started)
+    grad_started = gather_start(grad_buf, sems, 9)
+    for weight in weights:
+        weight.step()
+    relay = gather_forward(buf, sems, 6, started)
     gather_finish(buf, full, started, relay)
-    grad_relay = gather_forward(grad_buf, sems, 6, grad_started)
+    grad_relay = gather_forward(grad_buf, sems, 9, grad_started)
     gather_finish(grad_buf, grad_full, grad_started, grad_relay)
+    for _ in range(count.bit_length()):
+        for weight in weights:
+            weight.step()
 
 
 def middle_kernel(
@@ -253,54 +436,87 @@
     latent_sums(sums, grad_out[...] * mlp_out, 3, 4)
 
 
-def close_kernel(
-    term, normed_in, inverse_in, mod, grad_middle, tokens_grad, sums,
-    sbuf, near_in, out_buf, far_in, stats, sems,
+def tail_kernel(
+    count, orders,
+    term, normed_in, inverse_in, mod, grad_middle, two_sums, ada, biases, fc2, fc1, proj, qkv,
+    tokens_grad, grad_mod, cond_terms, bias_sums, fc2_out, fc1_out, proj_out, qkv_out,
+    sbuf, near_in, out_buf, far_in, stats, ones, grad_rows, cond_parts, bias_got,
+    fc2_acc, fc2_got, fc1_acc, fc1_got, proj_acc, proj_got, qkv_acc, qkv_got, sems, tok_sems,
 ):
     _, near, far, cross = partners()
+    t = lax.axis_index("tok")
     rows = normed_in.shape[0]
     mods = mod[...]
-    greet(near, far, cross)
+    lat = mods.shape[1]
+    each = count - 1
+    greet_all(count)
     started = scatter_start(term, sbuf, near_in, sems, 0)
+    bias_copies = [
+        push_tok(biases, bias_got.at[step - 1], tok_sems, 6 * each + step - 1, (t + step) % count)
+        for step in range(1, count)
+    ]
+    for copy in bias_copies:
+        copy.start()
+    grads = [
+        RowScatter(fc2, fc2_out, fc2_acc, fc2_got, False, orders[0], tok_sems, 0),
+        RowScatter(fc1, fc1_out, fc1_acc, fc1_got, False, orders[1], tok_sems, each),
+        RowScatter(proj, proj_out, proj_acc, proj_got, False, orders[1], tok_sems, 2 * each),
+        RowScatter(qkv, qkv_out, qkv_acc, qkv_got, True, orders[0], tok_sems, 3 * each),
+    ]
     crossing = scatter_cross(sbuf, near_in, out_buf, far_in, sems, 0, started)
     grad_hidden = scatter_finish(sbuf, near_in, far_in, started, crossing)
     normed = normed_in[...]
+    latent_sums(ones, grad_hidden, 0, 2)
+    latent_sums(ones, grad_hidden * normed, 1, 2)
+    for l in range(lat):
+        one, two = l * 2, l * 4
+        kept = (
+            ones[one : one + 1],
+            ones[one + 1 : one + 2],
+            two_sums[two + 2 : two + 3],
+            two_sums[two : two + 1],
+            two_sums[two + 1 : two + 2],
+            two_sums[two + 3 : two + 4],
+        )
+        for which in range(6):
+            grad_mod[t, which, l : l + 1] = kept[which]
+    mod_copies = send_all(grad_mod.at[t], grad_mod.at[t], tok_sems, 4 * each, count)
     tokens_grad[...] = grad_middle[...] + norm_grad(
         grad_hidden * (1.0 + spread(mods, 1, rows)), normed, inverse_in[...], stats, sems, 3
     )
-    latent_sums(sums, grad_hidden, 0, 2)
-    latent_sums(sums, grad_hidden * normed, 1, 2)
-
-
-def mod_kernel(count, term, bias, out, recv, sems):
-    t = lax.axis_index("tok")
-    barrier = pltpu.get_barrier_semaphore()
-    for step in range(1, count):
-        pl.semaphore_signal(
-            barrier, inc=1, device_id={"tok": (t + step) % count}, device_id_type=MESH
+    for grad in grads[:2]:
+        grad.step()
+    wait_all(mod_copies)
+    total = None
+    for which in range(6):
+        for owner in range(count):
+            grad_rows[which, owner * lat : (owner + 1) * lat] = grad_mod[owner, which]
+        piece = lax.dot_general(
+            grad_rows[which].astype(BF16), ada[which], (((1,), (1,)), ((), ())),
+            preferred_element_type=F32,
         )
-    pl.semaphore_wait(barrier, count - 1)
-    copies = []
-    for step in range(1, count):
-        peer = (t + step) % count
-        copies.append(
-            pltpu.make_async_remote_copy(
-                src_ref=term.at[peer],
-                dst_ref=recv.at[step - 1],
-                send_sem=sems.at[0, step - 1],
-                recv_sem=sems.at[1, step - 1],
-                device_id={"tok": peer},
-                device_id_type=MESH,
-            )
-        )
+        total = piece if total is None else total + piece
+    cond_parts[0] = total
+    copies = [
+        push(cond_parts.at[0], cond_parts.at[slot], sems, 5 + slot, peer)
+        for slot, peer in ((1, near), (2, far), (3, cross))
+    ]
     for copy in copies:
         copy.start()
-    for copy in copies:
-        copy.wait()
-    out[...] = term[t] + jnp.sum(recv[...], 0) + bias[...]
-
-
-def call(kernel, collective_id, outs, scratch, sem_count, *args):
+    for grad in grads[2:]:
+        grad.step()
+    wait_all(copies)
+    cond_terms[t] = (cond_parts[0] + cond_parts[1]) + (cond_parts[2] + cond_parts[3])
+    cond_copies = send_all(cond_terms.at[t], cond_terms.at[t], tok_sems, 5 * each, count)
+    for _ in range(count.bit_length()):
+        for grad in grads:
+            grad.step()
+    wait_all(bias_copies)
+    bias_sums[...] = biases[...] + jnp.sum(bias_got[...], 0)
+    wait_all(cond_copies)
+
+
+def call(kernel, collective_id, outs, scratch, sem_counts, *args):
     out_shape = [jax.ShapeDtypeStruct(shape, dtype) for shape, dtype in outs]
     return pl.pallas_call(
         kernel,
@@ -308,56 +524,11 @@
         in_specs=[VMEM] * len(args),
         out_specs=[VMEM] * len(outs),
         scratch_shapes=[pltpu.VMEM(shape, dtype) for shape, dtype in scratch]
-        + [pltpu.SemaphoreType.DMA((2, sem_count))],
+        + [pltpu.SemaphoreType.DMA((2, count)) for count in sem_counts],
         compiler_params=pltpu.CompilerParams(
             collective_id=collective_id, has_side_effects=True, vmem_limit_bytes=40 * 2**20
         ),
     )(*args)
-
-
-def bits_of(count):
-    return [count >> (i + 1) for i in range(count.bit_length() - 1)]
-
-
-def pick(values, axis, at):
-    return jnp.where(
-        at == 0, lax.index_in_dim(values, 0, axis, False), lax.index_in_dim(values, 1, axis, False)
-    )
-
-
-def gather_rows(block, row_axis, count, order):
-    t = lax.axis_index("tok")
-    bits = bits_of(count)
-    seen = []
-    held = block
-    for bit in [bits[i] for i in order]:
-        other = lax.ppermute(held, "tok", [(i, i ^ bit) for i in range(count)])
-        axis = row_axis + sum(1 for b in seen if b > bit)
-        low = (t // bit) % 2 == 0
-        held = jnp.stack(
-            [jnp.where(low, held, other), jnp.where(low, other, held)], axis
-        )
-        seen.append(bit)
-    shape = list(block.shape)
-    shape[row_axis] *= count
-    return held.reshape(shape)
-
-
-def scatter_rows(grad, row_axis, count, order):
-    t = lax.axis_index("tok")
-    bits = bits_of(count)
-    shape = list(grad.shape)
-    rows = shape[row_axis] // count
-    held = grad.reshape(shape[:row_axis] + [2] * len(bits) + [rows] + shape[row_axis + 1 :])
-    left = list(bits)
-    for bit in [bits[i] for i in order]:
-        axis = row_axis + left.index(bit)
-        mine = (t // bit) % 2
-        sent = pick(held, axis, 1 - mine).astype(BF16)
-        got = lax.ppermute(sent, "tok", [(i, i ^ bit) for i in range(count)])
-        held = pick(held, axis, mine).astype(F32) + got.astype(F32)
-        left.remove(bit)
-    return held
 
 
 def per_device(
@@ -383,43 +554,18 @@
     seq_len = rows // lat
     head_count = width // HEAD_DIM
     score_scale = HEAD_DIM ** (-0.5)
-    feat_at, tok_at = lax.axis_index("feat"), lax.axis_index("tok")
+    feat_at = lax.axis_index("feat")
     offset = feat_at * width
     head_shape = (lat, seq_len, head_count, HEAD_DIM)
     part = ada_weight.shape[1]
-    levels = len(bits_of(tok_count))
-    down = list(range(levels))
-    mixed = [levels - 1] + list(range(levels - 1))
+    bits = [tok_count >> (i + 1) for i in range(tok_count.bit_length() - 1)]
+    gather_orders = (bits, bits[-1:] + bits[:-1])
+    scatter_orders = tuple(order[::-1] for order in gather_orders)
+    lanes = -(-(width + 1) // 128) * 128
+    every = tok_count * lat
 
     waves = lax.dynamic_slice_in_dim(time_features(timesteps, D), offset, width, 1)
     condition = jnp.take(class_table, labels, axis=1).T.astype(F32) + waves
-    cond_all = lax.all_gather(condition, ("tok", "feat"), axis=0, tiled=False)
-    cond_all = (
-        cond_all.reshape(tok_count, FEAT, lat, width)
-        .transpose(0, 2, 1, 3)
-        .reshape(tok_count * lat, D)
-    )
-    labels_all = lax.all_gather(labels, "tok", axis=0, tiled=True)
-    qkv_full = gather_rows(qkv_weight, 1, tok_count, down)
-    proj_full = gather_rows(proj_weight, 0, tok_count, mixed)
-    fc1_full = gather_rows(fc1_weight, 0, tok_count, mixed)
-    fc2_full = gather_rows(fc2_weight, 0, tok_count, down)
-
-    cond_rows = jax.nn.silu(
-        lax.dynamic_slice_in_dim(cond_all, tok_at * part, part, 1)
-    ).astype(BF16)
-    mod_term = jnp.einsum("lk,jkc->ljc", cond_rows, ada_weight, preferred_element_type=F32)
-    mod_term = mod_term.reshape(tok_count, lat * 6, width)
-    (mod,) = call(
-        partial(mod_kernel, tok_count),
-        0,
-        [((lat * 6, width), F32)],
-        [((tok_count - 1, lat * 6, width), F32)],
-        tok_count - 1,
-        mod_term,
-        jnp.tile(ada_bias, (lat, 1)),
-    )
-
     own_f32 = ((rows, width), F32)
     own_low = ((rows, width), BF16)
     one_f32 = ((rows, 1), F32)
@@ -429,18 +575,47 @@
     stats = ((FEAT, 8, rows), F32)
     scatter_bufs = [buf, ((2, rows, width), BF16), own_low, own_low]
 
+    cond_sent = jnp.concatenate(
+        [condition, labels.astype(F32)[:, None], jnp.zeros((lat, lanes - width - 1), F32)], 1
+    )
+    mod_shape = ((6, lat, width), F32)
+    inner = fc1_bias.shape[0]
+    small = (tok_count, part, width)
+    large = (tok_count, part, inner)
     field_in = tokens.T
     grad_out = cotangent.T
-    full_one, grad_mlp_full, normed_one, inverse_one, fc2_bias_grad = call(
-        open_kernel,
-        1,
-        [full_low, full_low, own_f32, one_f32, line],
-        [buf, buf, stats],
-        9,
+    (
+        full_one, grad_mlp_full, normed_one, inverse_one, fc2_bias_grad, mod, cond_all, cond_rows,
+        qkv_full, proj_full, fc1_full, fc2_full,
+    ) = call(
+        partial(head_kernel, tok_count, gather_orders),
+        0,
+        [
+            full_low, full_low, own_f32, one_f32, line, mod_shape,
+            ((tok_count, FEAT, lat, lanes), F32), ((every, part), BF16),
+            ((3,) + small, BF16), (small, BF16), (large, BF16), (large, BF16),
+        ],
+        [
+            buf, buf, stats, ((FEAT, every, lanes), F32),
+            ((tok_count, 6, lat, width), F32), ((tok_count - 1, 6, lat, width), F32),
+        ],
+        (12, 6 * (tok_count - 1)),
         field_in,
-        mod,
         grad_out,
-    )
+        cond_sent,
+        ada_weight,
+        ada_bias[:, None],
+        qkv_weight,
+        proj_weight,
+        fc1_weight,
+        fc2_weight,
+    )
+    qkv_full = qkv_full.reshape(3, D, width)
+    proj_full = proj_full.reshape(D, width)
+    fc1_full = fc1_full.reshape(D, inner)
+    fc2_full = fc2_full.reshape(D, inner)
+    cond_all = cond_all.transpose(0, 2, 1, 3).reshape(every, FEAT, lanes)
+    labels_all = cond_all[:, 0, width].astype(jnp.int32)
     projected = jnp.einsum("rk,jkc->jrc", full_one, qkv_full, preferred_element_type=F32)
     queries = (projected[0] + qv_bias[0]).astype(BF16).reshape(head_shape)
     keys_low = projected[1].astype(BF16).reshape(head_shape)
@@ -461,7 +636,7 @@
         2,
         [own_f32, own_f32, own_f32, one_f32, full_low],
         scatter_bufs + [buf, stats],
-        9,
+        (9,),
         attn_term.astype(BF16),
         field_in,
         mod,
@@ -479,7 +654,7 @@
         3,
         [own_f32, full_low, own_f32, ((lat * 4, width), F32), line],
         scatter_bufs + scatter_bufs + [buf, stats],
-        12,
+        (12,),
         hidden_two_term.astype(BF16),
         mlp_term.astype(BF16),
         grad_out,
@@ -491,12 +666,9 @@
         attn_out,
     )
     fc2_grad = jnp.einsum("ro,rf->of", grad_mlp_full, act_low, preferred_element_type=F32)
-    fc2_shard = scatter_rows(fc2_grad.astype(BF16), 0, tok_count, down[::-1])
     fc1_bias_grad = jnp.sum(grad_pre, 0, dtype=F32)
     fc1_grad = jnp.einsum("rk,rf->kf", full_two, grad_pre, preferred_element_type=F32)
-    fc1_shard = scatter_rows(fc1_grad.astype(BF16), 0, tok_count, mixed[::-1])
     proj_grad = jnp.einsum("ro,rc->oc", grad_attn_full, attended, preferred_element_type=F32)
-    proj_shard = scatter_rows(proj_grad.astype(BF16), 0, tok_count, mixed[::-1])
     grad_attended = (
         jnp.dot(grad_attn_full, proj_full, preferred_element_type=F32)
         .astype(BF16)
@@ -523,42 +695,55 @@
         jnp.stack([grad_queries, grad_keys, grad_values]).astype(BF16).reshape(3, rows, width)
     )
     hidden_one_term = jnp.einsum("jrc,jkc->rk", grad_qkv, qkv_full, preferred_element_type=F32)
-    tokens_grad, one_sums = call(
-        close_kernel,
+    qkv_grad = jnp.einsum("rk,jrc->jkc", full_one, grad_qkv, preferred_element_type=F32)
+    bias_terms = jnp.concatenate(
+        [
+            jnp.sum(grad_qkv[0], 0, dtype=F32)[None],
+            jnp.sum(grad_qkv[2], 0, dtype=F32)[None],
+            proj_bias_grad,
+            fc1_bias_grad.reshape(-1, width),
+            fc2_bias_grad,
+        ]
+    )
+    small_parts = [((tok_count - 1, part, width), BF16)] * 2
+    large_parts = [((tok_count - 1, part, inner), BF16)] * 2
+    (
+        tokens_grad, grad_mod_all, cond_terms, bias_sums, fc2_shard, fc1_shard, proj_shard, qkv_shard
+    ) = call(
+        partial(tail_kernel, tok_count, scatter_orders),
         4,
-        [own_f32, ((lat * 2, width), F32)],
-        scatter_bufs + [stats],
-        6,
+        [
+            own_f32, ((tok_count, 6, lat, width), F32), ((tok_count, every, part), F32),
+            (bias_terms.shape, F32),
+            ((part, inner), F32), ((part, inner), F32), ((part, width), F32), ((3, part, width), F32),
+        ],
+        scatter_bufs
+        + [
+            stats, ((lat * 2, width), F32), ((6, every, width), F32), ((FEAT, every, part), F32),
+            ((tok_count - 1,) + bias_terms.shape, F32),
+        ]
+        + large_parts + large_parts + small_parts
+        + [((3, tok_count - 1, part, width), BF16)] * 2,
+        (9, 7 * (tok_count - 1)),
         hidden_one_term.astype(BF16),
         normed_one,
         inverse_one,
         mod,
         grad_middle,
-    )
-    qkv_grad = jnp.einsum("rk,jrc->jkc", full_one, grad_qkv, preferred_element_type=F32)
-    qkv_shard = scatter_rows(qkv_grad.astype(BF16), 1, tok_count, down[::-1])
-    qv_bias_grad = jnp.stack([jnp.sum(grad_qkv[0], 0, dtype=F32), jnp.sum(grad_qkv[2], 0, dtype=F32)])
-
-    ones = one_sums.reshape(lat, 2, width)
-    twos = two_sums.reshape(lat, 4, width)
-    grad_mod = jnp.stack(
-        [ones[:, 0], ones[:, 1], twos[:, 2], twos[:, 0], twos[:, 1], twos[:, 3]], 1
-    ).astype(BF16)
-    bias_terms = jnp.concatenate(
-        [qv_bias_grad.reshape(-1), proj_bias_grad[0], fc1_bias_grad, fc2_bias_grad[0]]
-    )
-    bias_sums = lax.psum(bias_terms, "tok")
-    grad_mod_all = lax.all_gather(grad_mod, "tok", axis=0, tiled=True)
-    ada_bias_sum = jnp.sum(grad_mod_all, 0, dtype=F32)
+        two_sums,
+        ada_weight,
+        bias_terms,
+        fc2_grad.astype(BF16).reshape(large),
+        fc1_grad.astype(BF16).reshape(large),
+        proj_grad.astype(BF16).reshape(small),
+        qkv_grad.astype(BF16).reshape((3,) + small),
+    )
+    grad_mod_all = grad_mod_all.astype(BF16)
+    ada_bias_sum = jnp.sum(grad_mod_all, (0, 2), dtype=F32)
+    grad_mod_all = grad_mod_all.transpose(0, 2, 1, 3).reshape(every, 6, width)
     ada_shard = jnp.einsum("lk,ljc->jkc", cond_rows, grad_mod_all, preferred_element_type=F32)
-    cond_term = jnp.einsum("ljc,jkc->lk", grad_mod_all, ada_weight, preferred_element_type=F32)
-    cond_terms = lax.all_gather(cond_term, ("tok", "feat"), axis=0, tiled=False)
-    grad_cond_act = (
-        jnp.sum(cond_terms.reshape(tok_count, FEAT, tok_count * lat, part), 1)
-        .transpose(1, 0, 2)
-        .reshape(tok_count * lat, D)
-    )
-    own_cond = lax.dynamic_slice_in_dim(cond_all, offset, width, 1)
+    grad_cond_act = cond_terms.transpose(1, 0, 2).reshape(every, D)
+    own_cond = lax.dynamic_index_in_dim(cond_all, feat_at, 1, False)[:, :width]
     own_grad = lax.dynamic_slice_in_dim(grad_cond_act, offset, width, 1)
     grad_condition = jax.vjp(jax.nn.silu, own_cond)[1](own_grad)[0]
     class_count = class_table.shape[1]
@@ -566,7 +751,6 @@
         labels_all[:, None] == jnp.arange(class_count, dtype=jnp.int32)[None, :]
     ).astype(F32)
     class_sum = jnp.einsum("lc,lw->wc", one_hot, grad_condition, precision=lax.Precision.HIGHEST)
-    inner = fc1_bias.shape[0]
     return (
         output.T,
         tokens_grad.T,
@@ -574,13 +758,13 @@
         ada_shard,
         ada_bias_sum,
         qkv_shard,
-        bias_sums[: 2 * width].reshape(2, width),
+        bias_sums[:2],
         proj_shard,
-        bias_sums[2 * width : 3 * width],
+        bias_sums[2],
         fc1_shard,
-        bias_sums[3 * width : 3 * width + inner],
+        bias_sums[3:-1].reshape(-1),
         fc2_shard,
-        bias_sums[3 * width + inner :],
+        bias_sums[-1],
     )
 
 

time: 440 us -> 240 us (0.55); the launches traced: 432 us -> 240 us
  blocking collectives: 139 us -> 0 us
  Pallas kernels: 92.8 us -> 170 us
  waiting for transfers between devices: 53.3 us -> 0 us
  starting transfers between devices: 25.9 us -> 0 us
  other arithmetic: 30.4 us -> 5.6 us
  local copies, waits for them, and re-layouts: 58.5 us -> 35.3 us
    all_gather x3 -> x0, blocking collectives: 110 us -> none  [the longest x1 42.4 us: per_device(): cond_all = lax.all_gather(condition, ('tok', 'feat'), axis=0, tiled=False)]
    pallas_call x5 -> x4, Pallas kernels: 92.8 us -> 170 us  [call(): pl.pallas_call(kernel, out_shape=out_shape, in_specs=[VMEM] * len(args),...]
    ppermute x24 -> x0, waiting for transfers between devices: 53.3 us -> none  [the longest x12 35.8 us: scatter_rows(): got = lax.ppermute(sent, 'tok', [(i, i ^ bit) for i in range(count)])]
    ppermute x24 -> x0, starting transfers between devices: 25.9 us -> none  [the longest x12 15.8 us: gather_rows(): other = lax.ppermute(held, 'tok', [(i, i ^ bit) for i in range(count)])]
    psum x1 -> x0, blocking collectives: 23.4 us -> none  [per_device(): bias_sums = lax.psum(bias_terms, 'tok')]
    another operation x28 -> x0, other arithmetic: 14.7 us -> none  [the longest x24 14.7 us: gather_rows(): jnp.stack([jnp.where(low, held, other), jnp.where(low, other, held)], axis)]
    reshape x11 -> x4, local copies, waits for them, and re-layouts: 14.7 us -> 0.88 us  [the longest x1 0.67 us: per_device(): bias_sums[3:-1].reshape(-1)]
    add x12 -> x1, other arithmetic: 8.87 us -> 0.09 us  [per_device(): condition = jnp.take(class_table, labels, axis=1).T.astype(F32) + waves]
  transfers between devices with their start and end apart: 24 -> 0, of which waited for: 11 -> 0; matrix products, arithmetic and copies ran while one was open for 17% -> 0% of each run, Pallas kernels for 12% -> 0%
where the time goes in v2:
time: 240 us
  Pallas kernels  170 us (71%)
  local copies, waits for them, and re-layouts  35.3 us (15%)
  matrix products  27.8 us (12%)
  other arithmetic  5.6 us (2%)
    pallas_call x4, Pallas kernels, call(): pl.pallas_call(kernel, out_shape=out_shape, in_specs=[VMEM] * len(args),...  170 us
    unnamed x116, local copies, waits for them, and re-layouts  20.9 us

profile of v2, /device:TPU:0, one launch (start us, length us, event | category | flops | bytes accessed | tf_op | source)
XLA Modules:
  0.0 239.7 jit_solution(10265870715152307760)
XLA Ops:
  0.7 0.7 convert_element_type.105
  2.1 0.7 compare_select_fusion
  3.0 0.8 slice_reduce_fusion
  4.1 0.7 broadcast_in_dim.46.bias
  4.8 1.3 copy.79
  7.3 62.5 %shard_map.246 = (bf16[512,768]{1,0:T(8,128)(2,1)S(1)}, bf16[512,768]{1,0:T(8,128)(2,1)S(1)}, f32[512,192]{1,0:T(8,128)S(1)}, f32[512,1]{1,0:T(8,128)S(1)}, f32[...) custom-call(f32[512,192]{1,0:T(8,128)S(1)} %bitcast.96, ...), custom_call_target="tpu_custom_call" | custom-call | tf_op jit(solution)/shard_map/pallas_call | solution.py:521
  69.9 1.3 fusion.45
  71.3 0.7 copy.147
  72.0 0.9 convolution_bitcast_fusion
  73.0 0.9 fusion.57
  73.9 2.1 squeeze.21
  76.0 2.0 squeeze.20
  78.0 3.4 %fusion.65 = f32[512,768]{1,0:T(8,128)} fusion(bf16[512,768]{1,0:T(8,128)(2,1)} %copy-done.32, bf16[768,768]{1,0:T(8,128)(2,1)} %bitcast.114), kind=kOutput, calls=%fused_computation.105 | convolution fusion | flops 603979776 | bytes 3538944 | tf_op jit(solution)/shard_map/dot_general | solution.py:648
  81.5 2.8 %fusion.59 = (f32[2,3,256]{2,1,0:T(4,128)S(1)}, f32[2,3,256,256]{2,3,1,0:T(8,128)}) fusion(bf16[2,256,3,64]{1,0,3,2:T(2,128)(2,1)S(1)} %convert_element_type.109, f32[2,256,3,64]{1,0,3,2:T(2,128)} %squeeze.21, f32[3,64]{1,0:T(4,128)S(1)} %add.62), kind=kOutput, calls=%fused_computation.104 | convolution fusion | flops 51708160 | bytes 2169600 | tf_op jit(solution)/shard_map/sub | solution.py:627
  84.3 1.8 fusion.13
  86.9 23.0 %shard_map.247 = (f32[512,192]{1,0:T(8,128)S(1)}, f32[512,192]{1,0:T(8,128)S(1)}, f32[512,192]{1,0:T(8,128)S(1)}, f32[512,1]{1,0:T(8,128)S(1)}, bf16[512,768]{1,0:T(8,128)(2,1)S(1)}) custom-call(bf16[512,768]{1,0:T(8,128)(2,1)S(1)} %convolution_convert_fusion.5.term, f32[512,192]{1,0:T(8,128)S(1)} %bitcast.97, f32[6,2,192]{2,1,0:T(2,128)S(1)} %get-tuple-element.48.mod, ...), custom_call_target="tpu_custom_call" | custom-call | tf_op jit(solution)/shard_map/pallas_call | solution.py:521
  109.9 1.7 convert_reduce_fusion
  111.6 1.1 convolution_convert_fusion.3.mlp_term
  113.0 0.8 convolution_convert_fusion.4.term
  113.9 27.6 %shard_map.248 = (f32[512,192]{1,0:T(8,128)S(1)}, bf16[512,768]{1,0:T(8,128)(2,1)S(1)}, f32[512,192]{1,0:T(8,128)S(1)}, f32[8,192]{1,0:T(8,128)S(1)}, f32[1,192]{1,0:T(1,128)S(1)}) custom-call(bf16[512,768]{1,0:T(8,128)(2,1)S(1)} %convolution_convert_fusion.4.term, bf16[512,768]{1,0:T(8,128)(2,1)S(1)} %convolution_convert_fusion.3.mlp_term, ...), custom_call_target="tpu_custom_call" | custom-call | tf_op jit(solution)/shard_map/pallas_call | solution.py:521
  141.5 0.8 copy-done.6
  142.3 0.8 copy-done.11
  143.7 1.1 convolution_convert_fusion.7
  144.8 1.7 reshape.132
  146.6 0.9 copy.102
  148.0 2.0 convert_reduce_fusion.1
  150.5 3.1 %convolution_convert_fusion = bf16[768,768]{1,0:T(8,128)(2,1)} fusion(bf16[512,768]{1,0:T(8,128)(2,1)S(1)} %copy-done.35, bf16[512,768]{1,0:T(8,128)(2,1)} %copy-done.48), kind=kOutput, calls=%fused_computation.17 | convolution fusion | flops 604569600 | bytes 2752512 | tf_op jit(solution)/shard_map/rk,rf->kf/dot_general | solution.py:670
  153.7 2.0 convolution_convert_fusion.1
  156.5 0.7 copy-done.36
  158.8 1.7 bitcast_convert_fusion.term
  160.5 1.6 fusion.10
  162.0 1.6 copy.98
  163.7 1.3 copy-done.2
  165.0 1.1 copy-done.5
  166.1 1.0 copy-done.10
  167.1 1.0 copy-done.12
  168.2 0.9 copy-done.18
  169.1 56.5 %shard_map.249 = (f32[512,192]{1,0:T(8,128)S(1)}, f32[8,6,2,192]{3,2,1,0:T(2,128)S(1)}, f32[8,16,96]{2,1,0:T(8,128)S(1)}, f32[8,192]{1,0:T(8,128)S(1)}, f32[96,7...) custom-call(bf16[512,768]{1,0:T(8,128)(2,1)S(1)} %copy-done.5, ...), custom_call_target="tpu_custom_call" | custom-call | tf_op jit(solution)/shard_map/pallas_call | solution.py:521
  225.6 0.8 copy-done.8
  226.4 0.7 copy-done.13
  227.1 0.7 copy-done.15
  228.5 2.0 copy.103
  232.4 1.6 convert_reduce_fusion.3
  234.3 1.1 copy.104
  235.4 1.5 fusion.30
  236.9 0.7 copy.154
  238.3 0.7 copy.156
  239.0 0.7 copy.157
  (141 shorter events, 11.0 us)
Async XLA Ops:
  0.6 6.4 %copy-start.41 = (f32[192,512]{1,0:T(8,128)S(1)}, f32[192,512]{1,0:T(8,128)}, u32[]{:S(2)}) copy-start(f32[192,512]{1,0:T(8,128)} %param.29) | copy-start | bytes 1179652
  0.7 6.1 %copy-start.40 = (f32[192,512]{1,0:T(8,128)S(1)}, f32[192,512]{1,0:T(8,128)}, u32[]{:S(2)}) copy-start(f32[192,512]{1,0:T(8,128)} %param.15) | copy-start | bytes 1179652
  4.8 2.5 %copy-start = (bf16[6,96,192]{2,1,0:T(8,128)(2,1)S(1)}, bf16[6,96,192]{2,1,0:T(8,128)(2,1)}, u32[]{:S(2)}) copy-start(bf16[6,96,192]{2,1,0:T(8,128)(2,1)} %ada.3) | copy-start | bytes 663556
  4.8 2.5 %copy-start.19 = (bf16[3,96,192]{2,1,0:T(8,128)(2,1)S(1)}, bf16[3,96,192]{2,1,0:T(8,128)(2,1)}, u32[]{:S(2)}) copy-start(bf16[3,96,192]{2,1,0:T(8,128)(2,1)} %qkv.1) | copy-start | bytes 331780
  4.8 2.5 %copy-start.20 = (bf16[96,768]{1,0:T(8,128)(2,1)S(1)}, bf16[96,768]{1,0:T(8,128)(2,1)}, u32[]{:S(2)}) copy-start(bf16[96,768]{1,0:T(8,128)(2,1)} %fc1.1) | copy-start | bytes 442372
  4.8 2.5 %copy-start.21 = (bf16[96,768]{1,0:T(8,128)(2,1)S(1)}, bf16[96,768]{1,0:T(8,128)(2,1)}, u32[]{:S(2)}) copy-start(bf16[96,768]{1,0:T(8,128)(2,1)} %fc2.1) | copy-start | bytes 442372
  4.8 2.5 %copy-start.23 = (bf16[96,192]{1,0:T(8,128)(2,1)S(1)}, bf16[96,192]{1,0:T(8,128)(2,1)}, u32[]{:S(2)}) copy-start(bf16[96,192]{1,0:T(8,128)(2,1)} %proj.1) | copy-start | bytes 110596
  69.8 3.1 %copy-start.3 = (bf16[512,768]{1,0:T(8,128)(2,1)}, bf16[512,768]{1,0:T(8,128)(2,1)S(1)}, u32[]{:S(2)}) copy-start(bf16[512,768]{1,0:T(8,128)(2,1)S(1)} %get-tuple-element.46) | copy-start | bytes 2359300
  69.8 3.1 %copy-start.9 = (f32[512,192]{1,0:T(8,128)}, f32[512,192]{1,0:T(8,128)S(1)}, u32[]{:S(2)}) copy-start(f32[512,192]{1,0:T(8,128)S(1)} %get-tuple-element.57.normed_in) | copy-start | bytes 1179652
  69.8 3.1 %copy-start.17 = (f32[512,1]{1,0:T(8,128)}, f32[512,1]{1,0:T(8,128)S(1)}, u32[]{:S(2)}) copy-start(f32[512,1]{1,0:T(8,128)S(1)} %get-tuple-element.58.inverse_in) | copy-start | bytes 6148
  69.8 3.0 %copy-start.28 = (bf16[8,96,768]{2,1,0:T(8,128)(2,1)}, bf16[8,96,768]{2,1,0:T(8,128)(2,1)S(1)}, u32[]{:S(2)}) copy-start(bf16[8,96,768]{2,1,0:T(8,128)(2,1)S(1)} %get-tuple-element.50) | copy-start | bytes 3538948
  69.9 3.1 %copy-start.30 = (bf16[8,96,768]{2,1,0:T(8,128)(2,1)}, bf16[8,96,768]{2,1,0:T(8,128)(2,1)S(1)}, u32[]{:S(2)}) copy-start(bf16[8,96,768]{2,1,0:T(8,128)(2,1)S(1)} %get-tuple-element.44) | copy-start | bytes 3538948
  69.9 3.1 %copy-start.32 = (bf16[512,768]{1,0:T(8,128)(2,1)}, bf16[512,768]{1,0:T(8,128)(2,1)S(1)}, u32[]{:S(2)}) copy-start(bf16[512,768]{1,0:T(8,128)(2,1)S(1)} %get-tuple-element.43) | copy-start | bytes 2359300
  73.9 7.5 %copy-start.38 = (bf16[2,256,3,64]{1,0,3,2:T(2,128)(2,1)}, bf16[2,256,3,64]{1,0,3,2:T(2,128)(2,1)S(1)}, u32[]{:S(2)}) copy-start(bf16[2,256,3,64]{1,0,3,2:T(2,128)(2,1)S(1)} %convert_element_type.109) | copy-start | bytes 589828
  86.4 23.5 %copy-start.29 = (bf16[8,96,768]{2,1,0:T(8,128)(2,1)S(1)}, bf16[8,96,768]{2,1,0:T(8,128)(2,1)}, u32[]{:S(2)}) copy-start(bf16[8,96,768]{2,1,0:T(8,128)(2,1)} %copy-done.28) | copy-start | bytes 3538948
  86.4 23.5 %copy-start.46 = (f32[768]{0:T(1024)S(1)}, f32[768]{0:T(1024)}, u32[]{:S(2)}) copy-start(f32[768]{0:T(1024)} %param.26) | copy-start | bytes 9220
  86.4 23.5 %copy-start.47 = (f32[512,768]{1,0:T(8,128)S(1)}, f32[512,768]{1,0:T(8,128)}, u32[]{:S(2)}) copy-start(f32[512,768]{1,0:T(8,128)} %fusion.65) | copy-start | bytes 4718596
  109.9 1.7 copy-start.34
  109.9 1.7 copy-start.31
  111.6 1.1 copy-start.49
  111.6 1.4 copy-start.48
  113.0 0.8 copy-start.26
  141.5 0.8 copy-start.6
  142.3 0.8 copy-start.11
  143.7 2.8 %copy-start.7 = (f32[512,192]{1,0:T(8,128)S(1)}, f32[512,192]{1,0:T(8,128)}, u32[]{:S(2)}) copy-start(f32[512,192]{1,0:T(8,128)} %copy-done.6) | copy-start | bytes 1179652
  148.0 2.5 %copy-start.35 = (bf16[512,768]{1,0:T(8,128)(2,1)S(1)}, bf16[512,768]{1,0:T(8,128)(2,1)}, u32[]{:S(2)}) copy-start(bf16[512,768]{1,0:T(8,128)(2,1)} %copy-done.34) | copy-start | bytes 2359300
  150.5 3.1 %copy-start.33 = (bf16[512,768]{1,0:T(8,128)(2,1)S(1)}, bf16[512,768]{1,0:T(8,128)(2,1)}, u32[]{:S(2)}) copy-start(bf16[512,768]{1,0:T(8,128)(2,1)} %copy-done.32) | copy-start | bytes 2359300
  150.5 3.1 %copy-start.50 = (f32[512,768]{1,0:T(8,128)S(1)}, f32[512,768]{1,0:T(8,128)}, u32[]{:S(2)}) copy-start(f32[512,768]{1,0:T(8,128)} %copy-done.49) | copy-start | bytes 4718596
  153.6 2.0 copy-start.37
  153.6 2.0 copy-start.42
  153.7 2.0 copy-start.43
  156.2 1.0 copy-start.36
  156.2 1.4 copy-start.39
  158.7 1.7 copy-start.4
  162.0 1.6 copy-start.1
  162.0 1.6 copy-start.25
  163.7 1.3 copy-start.2
  165.0 1.1 copy-start.5
  166.1 1.0 copy-start.10
  167.1 1.0 copy-start.12
  168.2 0.9 copy-start.18
  225.6 0.8 copy-start.8
  226.4 0.7 copy-start.13
  227.1 0.7 copy-start.15
  228.5 7.0 %copy-start.44 = (f32[16,1,256]{2,0,1:T(8,128)S(1)}, f32[16,1,256]{2,0,1:T(8,128)}, u32[]{:S(2)}) copy-start(f32[16,1,256]{2,0,1:T(8,128)} %copy.147) | copy-start | bytes 49156
  228.5 7.0 %copy-start.45 = (s32[16]{0:T(128)S(1)}, s32[16]{0:T(128)}, u32[]{:S(2)}) copy-start(s32[16]{0:T(128)} %fusion.45) | copy-start | bytes 196
  230.5 6.4 %copy-start.16 = (f32[3,96,192]{2,1,0:T(8,128)S(1)}, f32[3,96,192]{2,1,0:T(8,128)}, u32[]{:S(2)}) copy-start(f32[3,96,192]{2,1,0:T(8,128)} %copy-done.15) | copy-start | bytes 663556
  234.0 4.2 %copy-start.14 = (f32[96,768]{1,0:T(8,128)S(1)}, f32[96,768]{1,0:T(8,128)}, u32[]{:S(2)}) copy-start(f32[96,768]{1,0:T(8,128)} %copy-done.13) | copy-start | bytes 884740
  (3 other events, 2.0 us)

commit v3 on v2

--- a/solution.py
+++ b/solution.py
@@ -219,16 +219,23 @@
         copy.wait()
 
 
-def block_at(ref, block, lead):
+def block_at(ref, block, lead, cols=None):
+    if cols is not None:
+        return ref.at[block, :, cols]
     return ref.at[:, block] if lead else ref.at[block]
 
 
+def halves(ref):
+    half = ref.shape[-1] // 2
+    return pl.ds(0, half), pl.ds(half, half)
+
+
 class RowGather:
-    def __init__(self, block, full, lead, order, sems, base):
+    def __init__(self, block, full, lead, order, sems, base, cols=None):
         t = lax.axis_index("tok")
         self.full, self.lead, self.order, self.sems, self.base = full, lead, list(order), sems, base
-        self.held, self.copies = [()], []
-        block_at(full, t, lead)[...] = block[...]
+        self.held, self.copies, self.cols = [()], [], cols
+        block_at(full, t, lead, cols)[...] = block[...] if cols is None else block[:, cols]
         self.send()
 
     def send(self):
@@ -236,7 +243,7 @@
         bit = self.order[0]
         self.copies = []
         for held in self.held:
-            view = block_at(self.full, flip(t, *held), self.lead)
+            view = block_at(self.full, flip(t, *held), self.lead, self.cols)
             self.copies.append(push_tok(view, view, self.sems, self.base, flip(t, bit)))
             self.base += 1
         for copy in self.copies:
@@ -253,11 +260,12 @@
 
 
 class RowScatter:
-    def __init__(self, grad, out, acc, recv, lead, order, sems, base):
+    def __init__(self, grad, out, acc, recv, lead, order, sems, base, cols=None):
         self.out, self.acc, self.recv, self.lead = out, acc, recv, lead
+        self.cols = cols
         self.order, self.sems, self.base = list(order), sems, base
         t = lax.axis_index("tok")
-        self.own = lambda held: block_at(grad, flip(t, *held), lead)
+        self.own = lambda held: block_at(grad, flip(t, *held), lead, cols)
         self.slot = 0
         self.send()
 
@@ -270,7 +278,7 @@
         self.copies = [
             push_tok(
                 self.own((bit,) + held),
-                block_at(self.recv, self.slot + at, self.lead),
+                block_at(self.recv, self.slot + at, self.lead, self.cols),
                 self.sems,
                 self.base + self.slot + at,
                 flip(t, bit),
@@ -287,25 +295,29 @@
         for at, held in enumerate(self.kept):
             self.copies[at].wait()
             slot = self.slot + at
-            total = self.own(held)[...].astype(F32) + block_at(self.recv, slot, self.lead)[
-                ...
-            ].astype(F32)
-            if len(self.order) == 1:
+            total = self.own(held)[...].astype(F32) + block_at(
+                self.recv, slot, self.lead, self.cols
+            )[...].astype(F32)
+            if len(self.order) == 1 and self.cols is None:
                 self.out[...] = total
+            elif len(self.order) == 1:
+                self.out[:, self.cols] = total
             else:
-                block_at(self.acc, slot, self.lead)[...] = total.astype(BF16)
+                block_at(self.acc, slot, self.lead, self.cols)[...] = total.astype(BF16)
             places[frozenset(held)] = slot
         self.slot += len(self.kept)
         self.order.pop(0)
-        self.own = lambda held: block_at(self.acc, places[frozenset(held)], self.lead)
+        self.own = lambda held: block_at(
+            self.acc, places[frozenset(held)], self.lead, self.cols
+        )
         if self.order:
             self.send()
 
 
 def head_kernel(
     count, orders,
-    x, grad_out, cond, ada, bias, qkv, proj, fc1, fc2,
-    full, grad_full, normed_out, inverse_out, fc2_sum, mod, cond_all, cond_act, qkv_full, proj_full, fc1_full, fc2_full,
+    x, grad_out, cond, ada, bias, qkv, proj, fc1,
+    full, grad_full, normed_out, inverse_out, fc2_sum, mod, cond_all, cond_act, qkv_full, proj_full, fc1_full,
     buf, grad_buf, stats, cond_rows, terms, got, sems, tok_sems,
 ):
     f, near, far, cross = partners()
@@ -326,8 +338,10 @@
     wait_all(shares)
     sharing = send_all(cond_all.at[t], cond_all.at[t], tok_sems, 4 * each, count)
     weights.append(RowGather(proj, proj_full, False, orders[1], tok_sems, each))
-    weights.append(RowGather(fc1, fc1_full, False, orders[1], tok_sems, 2 * each))
-    weights.append(RowGather(fc2, fc2_full, False, orders[0], tok_sems, 3 * each))
+    for at, cols in enumerate(halves(fc1)):
+        weights.append(
+            RowGather(fc1, fc1_full, False, orders[1 - at], tok_sems, (2 + at) * each, cols)
+        )
     values = x[...]
     mean, inverse = norm_stats(values, stats, sems, 3)
     normed = (values - mean) * inverse
@@ -380,17 +394,24 @@
 
 
 def middle_kernel(
-    term, x, mod, bias, attn_out, middle_out, normed_out, inverse_out, full,
-    sbuf, near_in, out_buf, far_in, buf, stats, sems,
+    count, orders,
+    term, x, mod, bias, fc2, fc2_full, attn_out, middle_out, normed_out, inverse_out, full,
+    sbuf, near_in, out_buf, far_in, buf, stats, sems, tok_sems,
 ):
     f, near, far, cross = partners()
     rows = x.shape[0]
     mods = mod[...]
-    greet(near, far, cross)
+    greet_all(count)
     started = scatter_start(term, sbuf, near_in, sems, 0)
+    weights = [
+        RowGather(fc2, fc2_full, False, orders[1 - at], tok_sems, at * (count - 1), cols)
+        for at, cols in enumerate(halves(fc2))
+    ]
     crossing = scatter_cross(sbuf, near_in, out_buf, far_in, sems, 0, started)
     attn = scatter_finish(sbuf, near_in, far_in, started, crossing) + bias[...]
     attn_out[...] = attn
+    for weight in weights:
+        weight.step()
     middle = x[...] + spread(mods, 2, rows) * attn
     middle_out[...] = middle
     mean, inverse = norm_stats(middle, stats, sems, 3)
@@ -399,20 +420,32 @@
     inverse_out[...] = inverse
     buf[f] = (normed * (1.0 + spread(mods, 4, rows)) + spread(mods, 3, rows)).astype(BF16)
     gathering = gather_start(buf, sems, 6)
+    for weight in weights:
+        weight.step()
     relay = gather_forward(buf, sems, 6, gathering)
     gather_finish(buf, full, gathering, relay)
+    for _ in range(count.bit_length()):
+        for weight in weights:
+            weight.step()
 
 
 def back_kernel(
-    term, mlp_term, grad_out, normed_in, inverse_in, mod, bias, middle, attn,
-    grad_middle_out, full, output, sums, proj_sum,
-    sbuf, near_in, out_buf, far_in, mbuf, mnear, mout, mfar, buf, stats, sems,
+    count, orders,
+    term, mlp_term, grad_out, normed_in, inverse_in, mod, bias, middle, attn, fc2,
+    fc2_out, grad_middle_out, full, output, sums, proj_sum,
+    sbuf, near_in, out_buf, far_in, mbuf, mnear, mout, mfar, buf, stats, fc2_acc, fc2_got, sems, tok_sems,
 ):
     f, near, far, cross = partners()
     rows = grad_out.shape[0]
     mods = mod[...]
-    greet(near, far, cross)
+    greet_all(count)
     started = scatter_start(term, sbuf, near_in, sems, 0)
+    grads = [
+        RowScatter(
+            fc2, fc2_out, fc2_acc, fc2_got, False, orders[at], tok_sems, at * (count - 1), cols
+        )
+        for at, cols in enumerate(halves(fc2))
+    ]
     mlp_started = scatter_start(mlp_term, mbuf, mnear, sems, 3)
     crossing = scatter_cross(sbuf, near_in, out_buf, far_in, sems, 0, started)
     grad_hidden = scatter_finish(sbuf, near_in, far_in, started, crossing)
@@ -424,6 +457,8 @@
     buf[f] = grad_attn
     gathering = gather_start(buf, sems, 9)
     mlp_crossing = scatter_cross(mbuf, mnear, mout, mfar, sems, 3, mlp_started)
+    for grad in grads:
+        grad.step()
     grad_middle_out[...] = grad_middle
     proj_sum[...] = jnp.sum(grad_attn.astype(F32), 0, keepdims=True)
     latent_sums(sums, grad_hidden, 0, 4)
@@ -431,17 +466,22 @@
     latent_sums(sums, grad_middle * attn[...], 2, 4)
     relay = gather_forward(buf, sems, 9, gathering)
     gather_finish(buf, full, gathering, relay)
+    for grad in grads:
+        grad.step()
     mlp_out = scatter_finish(mbuf, mnear, mfar, mlp_started, mlp_crossing) + bias[...]
     output[...] = middle[...] + spread(mods, 5, rows) * mlp_out
     latent_sums(sums, grad_out[...] * mlp_out, 3, 4)
+    for _ in range(count.bit_length()):
+        for grad in grads:
+            grad.step()
 
 
 def tail_kernel(
     count, orders,
-    term, normed_in, inverse_in, mod, grad_middle, two_sums, ada, biases, fc2, fc1, proj, qkv,
-    tokens_grad, grad_mod, cond_terms, bias_sums, fc2_out, fc1_out, proj_out, qkv_out,
+    term, normed_in, inverse_in, mod, grad_middle, two_sums, ada, biases, fc1, proj, qkv,
+    tokens_grad, grad_mod, cond_terms, bias_sums, fc1_out, proj_out, qkv_out,
     sbuf, near_in, out_buf, far_in, stats, ones, grad_rows, cond_parts, bias_got,
-    fc2_acc, fc2_got, fc1_acc, fc1_got, proj_acc, proj_got, qkv_acc, qkv_got, sems, tok_sems,
+    fc1_acc, fc1_got, proj_acc, proj_got, qkv_acc, qkv_got, sems, tok_sems,
 ):
     _, near, far, cross = partners()
     t = lax.axis_index("tok")
@@ -458,8 +498,9 @@
     for copy in bias_copies:
         copy.start()
     grads = [
-        RowScatter(fc2, fc2_out, fc2_acc, fc2_got, False, orders[0], tok_sems, 0),
-        RowScatter(fc1, fc1_out, fc1_acc, fc1_got, False, orders[1], tok_sems, each),
+        RowScatter(fc1, fc1_out, fc1_acc, fc1_got, False, orders[at], tok_sems, at * each, cols)
+        for at, cols in enumerate(halves(fc1))
+    ] + [
         RowScatter(proj, proj_out, proj_acc, proj_got, False, orders[1], tok_sems, 2 * each),
         RowScatter(qkv, qkv_out, qkv_acc, qkv_got, True, orders[0], tok_sems, 3 * each),
     ]
@@ -582,18 +623,20 @@
     inner = fc1_bias.shape[0]
     small = (tok_count, part, width)
     large = (tok_count, part, inner)
+    small_parts = [((tok_count - 1, part, width), BF16)] * 2
+    large_parts = [((tok_count - 1, part, inner), BF16)] * 2
     field_in = tokens.T
     grad_out = cotangent.T
     (
         full_one, grad_mlp_full, normed_one, inverse_one, fc2_bias_grad, mod, cond_all, cond_rows,
-        qkv_full, proj_full, fc1_full, fc2_full,
+        qkv_full, proj_full, fc1_full,
     ) = call(
         partial(head_kernel, tok_count, gather_orders),
         0,
         [
             full_low, full_low, own_f32, one_f32, line, mod_shape,
             ((tok_count, FEAT, lat, lanes), F32), ((every, part), BF16),
-            ((3,) + small, BF16), (small, BF16), (large, BF16), (large, BF16),
+            ((3,) + small, BF16), (small, BF16), (large, BF16),
         ],
         [
             buf, buf, stats, ((FEAT, every, lanes), F32),
@@ -608,12 +651,10 @@
         qkv_weight,
         proj_weight,
         fc1_weight,
-        fc2_weight,
     )
     qkv_full = qkv_full.reshape(3, D, width)
     proj_full = proj_full.reshape(D, width)
     fc1_full = fc1_full.reshape(D, inner)
-    fc2_full = fc2_full.reshape(D, inner)
     cond_all = cond_all.transpose(0, 2, 1, 3).reshape(every, FEAT, lanes)
     labels_all = cond_all[:, 0, width].astype(jnp.int32)
     projected = jnp.einsum("rk,jkc->jrc", full_one, qkv_full, preferred_element_type=F32)
@@ -631,17 +672,19 @@
     attended = jnp.einsum("lhqk,lkhd->lqhd", probs_low, values_low, preferred_element_type=F32)
     attended = attended.astype(BF16).reshape(rows, width)
     attn_term = jnp.einsum("rc,oc->ro", attended, proj_full, preferred_element_type=F32)
-    attn_out, middle, normed_two, inverse_two, full_two = call(
-        middle_kernel,
+    fc2_full, attn_out, middle, normed_two, inverse_two, full_two = call(
+        partial(middle_kernel, tok_count, gather_orders),
         2,
-        [own_f32, own_f32, own_f32, one_f32, full_low],
+        [(large, BF16), own_f32, own_f32, own_f32, one_f32, full_low],
         scatter_bufs + [buf, stats],
-        (9,),
+        (9, 2 * (tok_count - 1)),
         attn_term.astype(BF16),
         field_in,
         mod,
         proj_bias[None],
-    )
+        fc2_weight,
+    )
+    fc2_full = fc2_full.reshape(D, inner)
     pre_act = jnp.dot(full_two, fc1_full, preferred_element_type=F32) + fc1_bias
     act_value, gelu_back = jax.vjp(partial(jax.nn.gelu, approximate=True), pre_act)
     act_low = act_value.astype(BF16)
@@ -649,12 +692,13 @@
     grad_pre = gelu_back(grad_act)[0].astype(BF16)
     mlp_term = jnp.einsum("rf,of->ro", act_low, fc2_full, preferred_element_type=F32)
     hidden_two_term = jnp.einsum("rf,kf->rk", grad_pre, fc1_full, preferred_element_type=F32)
-    grad_middle, grad_attn_full, output, two_sums, proj_bias_grad = call(
-        back_kernel,
+    fc2_grad = jnp.einsum("ro,rf->of", grad_mlp_full, act_low, preferred_element_type=F32)
+    fc2_shard, grad_middle, grad_attn_full, output, two_sums, proj_bias_grad = call(
+        partial(back_kernel, tok_count, scatter_orders),
         3,
-        [own_f32, full_low, own_f32, ((lat * 4, width), F32), line],
-        scatter_bufs + scatter_bufs + [buf, stats],
-        (12,),
+        [((part, inner), F32), own_f32, full_low, own_f32, ((lat * 4, width), F32), line],
+        scatter_bufs + scatter_bufs + [buf, stats] + large_parts,
+        (12, 2 * (tok_count - 1)),
         hidden_two_term.astype(BF16),
         mlp_term.astype(BF16),
         grad_out,
@@ -664,8 +708,8 @@
         fc2_bias[None],
         middle,
         attn_out,
-    )
-    fc2_grad = jnp.einsum("ro,rf->of", grad_mlp_full, act_low, preferred_element_type=F32)
+        fc2_grad.astype(BF16).reshape(large),
+    )
     fc1_bias_grad = jnp.sum(grad_pre, 0, dtype=F32)
     fc1_grad = jnp.einsum("rk,rf->kf", full_two, grad_pre, preferred_element_type=F32)
     proj_grad = jnp.einsum("ro,rc->oc", grad_attn_full, attended, preferred_element_type=F32)
@@ -705,24 +749,22 @@
             fc2_bias_grad,
         ]
     )
-    small_parts = [((tok_count - 1, part, width), BF16)] * 2
-    large_parts = [((tok_count - 1, part, inner), BF16)] * 2
     (
-        tokens_grad, grad_mod_all, cond_terms, bias_sums, fc2_shard, fc1_shard, proj_shard, qkv_shard
+        tokens_grad, grad_mod_all, cond_terms, bias_sums, fc1_shard, proj_shard, qkv_shard
     ) = call(
         partial(tail_kernel, tok_count, scatter_orders),
         4,
         [
             own_f32, ((tok_count, 6, lat, width), F32), ((tok_count, every, part), F32),
             (bias_terms.shape, F32),
-            ((part, inner), F32), ((part, inner), F32), ((part, width), F32), ((3, part, width), F32),
+            ((part, inner), F32), ((part, width), F32), ((3, part, width), F32),
         ],
         scatter_bufs
         + [
             stats, ((lat * 2, width), F32), ((6, every, width), F32), ((FEAT, every, part), F32),
             ((tok_count - 1,) + bias_terms.shape, F32),
         ]
-        + large_parts + large_parts + small_parts
+        + large_parts + small_parts
         + [((3, tok_count - 1, part, width), BF16)] * 2,
         (9, 7 * (tok_count - 1)),
         hidden_one_term.astype(BF16),
@@ -733,7 +775,6 @@
         two_sums,
         ada_weight,
         bias_terms,
-        fc2_grad.astype(BF16).reshape(large),
         fc1_grad.astype(BF16).reshape(large),
         proj_grad.astype(BF16).reshape(small),
         qkv_grad.astype(BF16).reshape((3,) + small),

time: 240 us -> 231 us (0.963)
  Pallas kernels: 170 us -> 156 us
    pallas_call x4, Pallas kernels: 170 us -> 156 us  [call(): pl.pallas_call(kernel, out_shape=out_shape, in_specs=[VMEM] * len(args),...]
    dot_general x1, matrix products: 3.43 us -> 0.78 us  [per_device(): grad_act = jnp.dot(grad_mlp_full, fc2_full, preferred_element_type=F32)]
    unnamed x116 -> x128, local copies, waits for them, and re-layouts: 20.9 us -> 23 us
where the time goes in v3:
time: 231 us; the launch traced here: 230 us
  Pallas kernels  156 us (68%)
  local copies, waits for them, and re-layouts  37.4 us (16%)
  matrix products  29.6 us (13%)
  other arithmetic  5.57 us (2%)
    pallas_call x4, Pallas kernels, call(): pl.pallas_call(kernel, out_shape=out_shape, in_specs=[VMEM] * len(args),...  156 us
    unnamed x128, local copies, waits for them, and re-layouts  23 us

profile of v3, /device:TPU:0, one launch (start us, length us, event | category | flops | bytes accessed | tf_op | source)
XLA Modules:
  0.0 230.3 jit_solution(2605109112358424540)
XLA Ops:
  0.7 0.7 convert_element_type.105
  2.1 0.7 compare_select_fusion
  3.0 0.8 slice_reduce_fusion
  4.8 1.3 copy.79
  7.2 52.4 %shard_map.246 = (bf16[512,768]{1,0:T(8,128)(2,1)S(1)}, bf16[512,768]{1,0:T(8,128)(2,1)S(1)}, f32[512,192]{1,0:T(8,128)S(1)}, f32[512,1]{1,0:T(8,128)S(1)}, f32[...) custom-call(f32[512,192]{1,0:T(8,128)S(1)} %bitcast.96, ...), custom_call_target="tpu_custom_call" | custom-call | tf_op jit(solution)/shard_map/pallas_call | solution.py:562
  59.7 0.9 copy-done.39
  60.6 1.3 fusion.45
  62.5 0.9 convolution_bitcast_fusion
  63.5 0.9 fusion.57
  64.5 2.1 squeeze.21
  66.6 2.0 squeeze.20
  68.6 2.9 %fusion.59 = (f32[2,3,256]{2,1,0:T(4,128)S(1)}, f32[2,3,256,256]{2,3,1,0:T(8,128)}) fusion(bf16[2,256,3,64]{1,0,3,2:T(2,128)(2,1)S(1)} %convert_element_type.109, f32[2,256,3,64]{1,0,3,2:T(2,128)} %squeeze.21, f32[3,64]{1,0:T(4,128)S(1)} %add.62), kind=kOutput, calls=%fused_computation.104 | convolution fusion | flops 51708160 | bytes 2169600 | tf_op jit(solution)/shard_map/sub | solution.py:668
  71.4 1.8 fusion.13
  74.2 1.3 convolution_convert_fusion.5.term
  75.6 28.7 %shard_map.247 = (bf16[8,96,768]{2,1,0:T(8,128)(2,1)S(1)}, f32[512,192]{1,0:T(8,128)S(1)}, f32[512,192]{1,0:T(8,128)S(1)}, f32[512,192]{1,0:T(8,128)S(1)}, f32[5...) custom-call(bf16[512,768]{1,0:T(8,128)(2,1)S(1)} %convolution_convert_fusion.5.term, f32[512,192]{1,0:T(8,128)S(1)} %bitcast.97, ...), custom_call_target="tpu_custom_call" | custom-call | tf_op jit(solution)/shard_map/pallas_call | solution.py:562
  104.4 0.8 fusion.65
  105.5 1.0 copy-done.38
  106.5 1.7 convert_reduce_fusion
  108.2 2.0 convolution_convert_fusion.3.mlp_term
  110.2 1.7 convolution_convert_fusion.4.term
  112.0 3.5 %convolution_convert_fusion = bf16[768,768]{1,0:T(8,128)(2,1)} fusion(bf16[512,768]{1,0:T(8,128)(2,1)} %copy-done.42, bf16[512,768]{1,0:T(8,128)(2,1)} %copy-done.54), kind=kOutput, calls=%fused_computation.17 | convolution fusion | flops 604569600 | bytes 2752512 | tf_op jit(solution)/shard_map/rk,rf->kf/dot_general | solution.py:714
  115.6 0.9 convolution_convert_fusion.1
  117.4 29.5 %shard_map.248 = (f32[96,768]{1,0:T(8,128)S(1)}, f32[512,192]{1,0:T(8,128)S(1)}, bf16[512,768]{1,0:T(8,128)(2,1)S(1)}, f32[512,192]{1,0:T(8,128)S(1)}, f32[8,192]{1,0:T(8,128)S(1)}, /*index=5*/f32[1,192]{1,0:T(1,128)S(1)}) custom-call(bf16[512,768]{1,0:T(8,128)(2,1)S(1)} %copy-done.3, bf16[512,768]{1,0:T(8,128)(2,1)S(1)} %copy-done.2, ...), custom_call_target="tpu_custom_call" | custom-call | tf_op jit(solution)/shard_map/pallas_call | solution.py:562
  147.0 0.8 copy-done.9
  147.8 0.8 copy-done.17
  149.1 1.1 convolution_convert_fusion.7
  150.3 1.7 reshape.133
  151.9 0.9 copy.102
  152.8 1.2 convolution_convert_fusion.6
  154.3 2.0 convert_reduce_fusion.1
  156.8 2.0 multiply_reduce_fusion
  161.4 1.7 bitcast_convert_fusion.term
  163.1 1.6 fusion.10
  164.7 1.6 copy.98
  166.4 1.1 copy-done.6
  167.5 1.0 copy-done.8
  168.5 1.0 copy-done.10
  169.6 0.9 copy-done.25
  170.5 45.7 %shard_map.249 = (f32[512,192]{1,0:T(8,128)S(1)}, f32[8,6,2,192]{3,2,1,0:T(2,128)S(1)}, f32[8,16,96]{2,1,0:T(8,128)S(1)}, f32[8,192]{1,0:T(8,128)S(1)}, f32[96,7...) custom-call(bf16[512,768]{1,0:T(8,128)(2,1)S(1)} %copy-done.6, f32[512,192]{1,0:T(8,128)S(1)} %copy-done.8, ...), custom_call_target="tpu_custom_call" | custom-call | tf_op jit(solution)/shard_map/pallas_call | solution.py:562
  216.2 0.8 copy-done.19
  217.0 0.7 copy-done.20
  219.1 2.0 copy.103
  223.0 1.6 convert_reduce_fusion.3
  224.9 1.1 copy.104
  226.0 1.5 fusion.30
  227.5 0.7 copy.154
  228.9 0.7 copy.156
  229.6 0.7 copy.157
  (153 shorter events, 14.1 us)
Async XLA Ops:
  0.6 6.3 %copy-start.48 = (f32[192,512]{1,0:T(8,128)S(1)}, f32[192,512]{1,0:T(8,128)}, u32[]{:S(2)}) copy-start(f32[192,512]{1,0:T(8,128)} %param.29) | copy-start | bytes 1179652
  0.7 6.1 %copy-start.47 = (f32[192,512]{1,0:T(8,128)S(1)}, f32[192,512]{1,0:T(8,128)}, u32[]{:S(2)}) copy-start(f32[192,512]{1,0:T(8,128)} %param.15) | copy-start | bytes 1179652
  4.8 2.5 %copy-start = (bf16[6,96,192]{2,1,0:T(8,128)(2,1)S(1)}, bf16[6,96,192]{2,1,0:T(8,128)(2,1)}, u32[]{:S(2)}) copy-start(bf16[6,96,192]{2,1,0:T(8,128)(2,1)} %ada.3) | copy-start | bytes 663556
  4.8 2.5 %copy-start.28 = (bf16[3,96,192]{2,1,0:T(8,128)(2,1)S(1)}, bf16[3,96,192]{2,1,0:T(8,128)(2,1)}, u32[]{:S(2)}) copy-start(bf16[3,96,192]{2,1,0:T(8,128)(2,1)} %qkv.1) | copy-start | bytes 331780
  4.8 2.5 %copy-start.29 = (bf16[96,768]{1,0:T(8,128)(2,1)S(1)}, bf16[96,768]{1,0:T(8,128)(2,1)}, u32[]{:S(2)}) copy-start(bf16[96,768]{1,0:T(8,128)(2,1)} %fc1.1) | copy-start | bytes 442372
  4.8 2.5 %copy-start.32 = (bf16[96,192]{1,0:T(8,128)(2,1)S(1)}, bf16[96,192]{1,0:T(8,128)(2,1)}, u32[]{:S(2)}) copy-start(bf16[96,192]{1,0:T(8,128)(2,1)} %proj.1) | copy-start | bytes 110596
  60.5 2.9 %copy-start.4 = (bf16[512,768]{1,0:T(8,128)(2,1)}, bf16[512,768]{1,0:T(8,128)(2,1)S(1)}, u32[]{:S(2)}) copy-start(bf16[512,768]{1,0:T(8,128)(2,1)S(1)} %get-tuple-element.45) | copy-start | bytes 2359300
  60.5 2.9 %copy-start.7 = (f32[512,192]{1,0:T(8,128)}, f32[512,192]{1,0:T(8,128)S(1)}, u32[]{:S(2)}) copy-start(f32[512,192]{1,0:T(8,128)S(1)} %get-tuple-element.57.normed_in) | copy-start | bytes 1179652
  60.5 2.9 %copy-start.24 = (f32[512,1]{1,0:T(8,128)}, f32[512,1]{1,0:T(8,128)S(1)}, u32[]{:S(2)}) copy-start(f32[512,1]{1,0:T(8,128)S(1)} %get-tuple-element.58.inverse_in) | copy-start | bytes 6148
  60.5 2.9 %copy-start.37 = (bf16[8,96,768]{2,1,0:T(8,128)(2,1)}, bf16[8,96,768]{2,1,0:T(8,128)(2,1)S(1)}, u32[]{:S(2)}) copy-start(bf16[8,96,768]{2,1,0:T(8,128)(2,1)S(1)} %get-tuple-element.50) | copy-start | bytes 3538948
  64.5 6.9 %copy-start.45 = (bf16[2,256,3,64]{1,0,3,2:T(2,128)(2,1)}, bf16[2,256,3,64]{1,0,3,2:T(2,128)(2,1)S(1)}, u32[]{:S(2)}) copy-start(bf16[2,256,3,64]{1,0,3,2:T(2,128)(2,1)S(1)} %convert_element_type.109) | copy-start | bytes 589828
  73.3 2.3 copy-start.30
  73.3 2.3 copy-start.35
  73.5 30.8 %copy-start.40 = (bf16[512,768]{1,0:T(8,128)(2,1)S(1)}, bf16[512,768]{1,0:T(8,128)(2,1)}, u32[]{:S(2)}) copy-start(bf16[512,768]{1,0:T(8,128)(2,1)} %copy-done.39) | copy-start | bytes 2359300
  104.3 0.9 copy-start.13
  104.3 1.1 copy-start.15
  104.3 1.2 copy-start.26
  104.3 3.9 %copy-start.42 = (bf16[512,768]{1,0:T(8,128)(2,1)}, bf16[512,768]{1,0:T(8,128)(2,1)S(1)}, u32[]{:S(2)}) copy-start(bf16[512,768]{1,0:T(8,128)(2,1)S(1)} %get-tuple-element.49) | copy-start | bytes 2359300
  104.3 2.1 copy-start.38
  104.3 2.1 copy-start.53
  108.2 2.0 copy-start.55
  108.2 2.0 copy-start.54
  112.0 3.5 %copy-start.41 = (bf16[512,768]{1,0:T(8,128)(2,1)S(1)}, bf16[512,768]{1,0:T(8,128)(2,1)}, u32[]{:S(2)}) copy-start(bf16[512,768]{1,0:T(8,128)(2,1)} %copy-done.39) | copy-start | bytes 2359300
  112.0 3.5 %copy-start.56 = (f32[512,768]{1,0:T(8,128)S(1)}, f32[512,768]{1,0:T(8,128)}, u32[]{:S(2)}) copy-start(f32[512,768]{1,0:T(8,128)} %copy-done.55) | copy-start | bytes 4718596
  115.5 1.1 copy-start.2
  115.5 1.4 copy-start.3
  115.5 1.5 copy-start.12
  115.5 1.7 copy-start.14
  115.5 1.8 copy-start.16
  115.5 1.9 copy-start.27
  115.5 1.8 copy-start.36
  149.1 2.8 %copy-start.18 = (f32[512,192]{1,0:T(8,128)S(1)}, f32[512,192]{1,0:T(8,128)}, u32[]{:S(2)}) copy-start(f32[512,192]{1,0:T(8,128)} %copy-done.17) | copy-start | bytes 1179652
  154.3 2.5 %copy-start.49 = (f32[2,256,3,64]{1,0,3,2:T(2,128)S(1)}, f32[2,256,3,64]{1,0,3,2:T(2,128)}, u32[]{:S(2)}) copy-start(f32[2,256,3,64]{1,0,3,2:T(2,128)} %squeeze.20) | copy-start | bytes 1179652
  154.3 2.5 %copy-start.50 = (bf16[2,256,3,64]{1,0,3,2:T(2,128)(2,1)S(1)}, bf16[2,256,3,64]{1,0,3,2:T(2,128)(2,1)}, u32[]{:S(2)}) copy-start(bf16[2,256,3,64]{1,0,3,2:T(2,128)(2,1)} %reshape.133) | copy-start | bytes 589828
  156.8 2.0 copy-start.44
  158.8 1.0 copy-start.43
  158.8 1.4 copy-start.46
  161.4 1.7 copy-start.5
  164.7 1.6 copy-start.1
  164.7 1.6 copy-start.34
  166.3 1.1 copy-start.6
  167.5 1.0 copy-start.8
  168.5 1.0 copy-start.10
  169.6 0.9 copy-start.25
  219.1 7.0 %copy-start.51 = (f32[16,1,256]{2,0,1:T(8,128)S(1)}, f32[16,1,256]{2,0,1:T(8,128)}, u32[]{:S(2)}) copy-start(f32[16,1,256]{2,0,1:T(8,128)} %copy.147) | copy-start | bytes 49156
  219.1 7.0 %copy-start.52 = (s32[16]{0:T(128)S(1)}, s32[16]{0:T(128)}, u32[]{:S(2)}) copy-start(s32[16]{0:T(128)} %fusion.45) | copy-start | bytes 196
  221.1 6.4 %copy-start.23 = (f32[3,96,192]{2,1,0:T(8,128)S(1)}, f32[3,96,192]{2,1,0:T(8,128)}, u32[]{:S(2)}) copy-start(f32[3,96,192]{2,1,0:T(8,128)} %copy-done.22) | copy-start | bytes 663556
  224.6 4.2 %copy-start.21 = (f32[96,768]{1,0:T(8,128)S(1)}, f32[96,768]{1,0:T(8,128)}, u32[]{:S(2)}) copy-start(f32[96,768]{1,0:T(8,128)} %copy-done.20) | copy-start | bytes 884740
  (9 other events, 6.8 us)

commit v4 on v3

--- a/solution.py
+++ b/solution.py
@@ -371,13 +371,13 @@
     ]
     for copy in copies:
         copy.start()
-    for weight in weights:
-        weight.step()
     wait_all(copies)
     mod[...] = terms[t] + jnp.sum(got[...], 0) + bias[...]
     mods = mod[...]
     buf[f] = (normed * (1.0 + spread(mods, 1, rows)) + spread(mods, 0, rows)).astype(BF16)
     started = gather_start(buf, sems, 6)
+    for weight in weights:
+        weight.step()
     grad_mlp = (grad_out[...] * spread(mods, 5, rows)).astype(BF16)
     fc2_sum[...] = jnp.sum(grad_mlp.astype(F32), 0, keepdims=True)
     grad_buf[f] = grad_mlp

time: 231 us -> 233 us (level)
  no operation moved by 1% of the time
where the time goes in v4:
time: 233 us; the launch traced here: 232 us
  Pallas kernels  158 us (68%)
  local copies, waits for them, and re-layouts  37.4 us (16%)
  matrix products  29.6 us (13%)
  other arithmetic  5.57 us (2%)
    pallas_call x4, Pallas kernels, call(): pl.pallas_call(kernel, out_shape=out_shape, in_specs=[VMEM] * len(args),...  158 us
    unnamed x128, local copies, waits for them, and re-layouts  23 us

profile of v4, /device:TPU:0, one launch (start us, length us, event | category | flops | bytes accessed | tf_op | source)
XLA Modules:
  0.0 231.8 jit_solution(16259309920255593719)
XLA Ops:
  0.7 0.7 convert_element_type.105
  2.1 0.7 compare_select_fusion
  3.0 0.8 slice_reduce_fusion
  4.8 1.3 copy.79
  7.2 54.3 %shard_map.246 = (bf16[512,768]{1,0:T(8,128)(2,1)S(1)}, bf16[512,768]{1,0:T(8,128)(2,1)S(1)}, f32[512,192]{1,0:T(8,128)S(1)}, f32[512,1]{1,0:T(8,128)S(1)}, f32[...) custom-call(f32[512,192]{1,0:T(8,128)S(1)} %bitcast.96, ...), custom_call_target="tpu_custom_call" | custom-call | tf_op jit(solution)/shard_map/pallas_call | solution.py:562
  61.6 0.9 copy-done.39
  62.5 1.3 fusion.45
  64.5 0.9 convolution_bitcast_fusion
  65.4 0.9 fusion.57
  66.4 2.1 squeeze.21
  68.5 2.0 squeeze.20
  70.5 2.9 %fusion.59 = (f32[2,3,256]{2,1,0:T(4,128)S(1)}, f32[2,3,256,256]{2,3,1,0:T(8,128)}) fusion(bf16[2,256,3,64]{1,0,3,2:T(2,128)(2,1)S(1)} %convert_element_type.109, f32[2,256,3,64]{1,0,3,2:T(2,128)} %squeeze.21, f32[3,64]{1,0:T(4,128)S(1)} %add.62), kind=kOutput, calls=%fused_computation.104 | convolution fusion | flops 51708160 | bytes 2169600 | tf_op jit(solution)/shard_map/sub | solution.py:668
  73.3 1.8 fusion.13
  76.1 1.3 convolution_convert_fusion.5.term
  77.5 28.2 %shard_map.247 = (bf16[8,96,768]{2,1,0:T(8,128)(2,1)S(1)}, f32[512,192]{1,0:T(8,128)S(1)}, f32[512,192]{1,0:T(8,128)S(1)}, f32[512,192]{1,0:T(8,128)S(1)}, f32[5...) custom-call(bf16[512,768]{1,0:T(8,128)(2,1)S(1)} %convolution_convert_fusion.5.term, f32[512,192]{1,0:T(8,128)S(1)} %bitcast.97, ...), custom_call_target="tpu_custom_call" | custom-call | tf_op jit(solution)/shard_map/pallas_call | solution.py:562
  105.8 0.8 fusion.65
  106.9 1.0 copy-done.38
  107.9 1.7 convert_reduce_fusion
  109.6 2.0 convolution_convert_fusion.3.mlp_term
  111.6 1.7 convolution_convert_fusion.4.term
  113.4 3.5 %convolution_convert_fusion = bf16[768,768]{1,0:T(8,128)(2,1)} fusion(bf16[512,768]{1,0:T(8,128)(2,1)} %copy-done.42, bf16[512,768]{1,0:T(8,128)(2,1)} %copy-done.54), kind=kOutput, calls=%fused_computation.17 | convolution fusion | flops 604569600 | bytes 2752512 | tf_op jit(solution)/shard_map/rk,rf->kf/dot_general | solution.py:714
  117.0 0.9 convolution_convert_fusion.1
  118.8 29.9 %shard_map.248 = (f32[96,768]{1,0:T(8,128)S(1)}, f32[512,192]{1,0:T(8,128)S(1)}, bf16[512,768]{1,0:T(8,128)(2,1)S(1)}, f32[512,192]{1,0:T(8,128)S(1)}, f32[8,192]{1,0:T(8,128)S(1)}, /*index=5*/f32[1,192]{1,0:T(1,128)S(1)}) custom-call(bf16[512,768]{1,0:T(8,128)(2,1)S(1)} %copy-done.3, bf16[512,768]{1,0:T(8,128)(2,1)S(1)} %copy-done.2, ...), custom_call_target="tpu_custom_call" | custom-call | tf_op jit(solution)/shard_map/pallas_call | solution.py:562
  148.7 0.8 copy-done.9
  149.5 0.8 copy-done.17
  150.9 1.1 convolution_convert_fusion.7
  152.0 1.7 reshape.133
  153.7 0.9 copy.102
  154.6 1.2 convolution_convert_fusion.6
  156.1 2.0 convert_reduce_fusion.1
  158.5 2.0 multiply_reduce_fusion
  163.2 1.7 bitcast_convert_fusion.term
  164.9 1.6 fusion.10
  166.5 1.6 copy.98
  168.1 1.1 copy-done.6
  169.2 1.0 copy-done.8
  170.3 1.0 copy-done.10
  171.3 0.9 copy-done.25
  172.3 45.4 %shard_map.249 = (f32[512,192]{1,0:T(8,128)S(1)}, f32[8,6,2,192]{3,2,1,0:T(2,128)S(1)}, f32[8,16,96]{2,1,0:T(8,128)S(1)}, f32[8,192]{1,0:T(8,128)S(1)}, f32[96,7...) custom-call(bf16[512,768]{1,0:T(8,128)(2,1)S(1)} %copy-done.6, f32[512,192]{1,0:T(8,128)S(1)} %copy-done.8, ...), custom_call_target="tpu_custom_call" | custom-call | tf_op jit(solution)/shard_map/pallas_call | solution.py:562
  217.7 0.8 copy-done.19
  218.5 0.7 copy-done.20
  220.6 2.0 copy.103
  224.5 1.6 convert_reduce_fusion.3
  226.5 1.1 copy.104
  227.6 1.5 fusion.30
  229.0 0.7 copy.154
  230.4 0.7 copy.156
  231.1 0.7 copy.157
  (153 shorter events, 14.1 us)
Async XLA Ops:
  0.6 6.3 %copy-start.48 = (f32[192,512]{1,0:T(8,128)S(1)}, f32[192,512]{1,0:T(8,128)}, u32[]{:S(2)}) copy-start(f32[192,512]{1,0:T(8,128)} %param.29) | copy-start | bytes 1179652
  0.7 6.1 %copy-start.47 = (f32[192,512]{1,0:T(8,128)S(1)}, f32[192,512]{1,0:T(8,128)}, u32[]{:S(2)}) copy-start(f32[192,512]{1,0:T(8,128)} %param.15) | copy-start | bytes 1179652
  4.8 2.5 %copy-start = (bf16[6,96,192]{2,1,0:T(8,128)(2,1)S(1)}, bf16[6,96,192]{2,1,0:T(8,128)(2,1)}, u32[]{:S(2)}) copy-start(bf16[6,96,192]{2,1,0:T(8,128)(2,1)} %ada.3) | copy-start | bytes 663556
  4.8 2.5 %copy-start.28 = (bf16[3,96,192]{2,1,0:T(8,128)(2,1)S(1)}, bf16[3,96,192]{2,1,0:T(8,128)(2,1)}, u32[]{:S(2)}) copy-start(bf16[3,96,192]{2,1,0:T(8,128)(2,1)} %qkv.1) | copy-start | bytes 331780
  4.8 2.5 %copy-start.29 = (bf16[96,768]{1,0:T(8,128)(2,1)S(1)}, bf16[96,768]{1,0:T(8,128)(2,1)}, u32[]{:S(2)}) copy-start(bf16[96,768]{1,0:T(8,128)(2,1)} %fc1.1) | copy-start | bytes 442372
  4.8 2.5 %copy-start.32 = (bf16[96,192]{1,0:T(8,128)(2,1)S(1)}, bf16[96,192]{1,0:T(8,128)(2,1)}, u32[]{:S(2)}) copy-start(bf16[96,192]{1,0:T(8,128)(2,1)} %proj.1) | copy-start | bytes 110596
  62.5 2.9 %copy-start.4 = (bf16[512,768]{1,0:T(8,128)(2,1)}, bf16[512,768]{1,0:T(8,128)(2,1)S(1)}, u32[]{:S(2)}) copy-start(bf16[512,768]{1,0:T(8,128)(2,1)S(1)} %get-tuple-element.45) | copy-start | bytes 2359300
  62.5 2.9 %copy-start.7 = (f32[512,192]{1,0:T(8,128)}, f32[512,192]{1,0:T(8,128)S(1)}, u32[]{:S(2)}) copy-start(f32[512,192]{1,0:T(8,128)S(1)} %get-tuple-element.57.normed_in) | copy-start | bytes 1179652
  62.5 2.9 %copy-start.24 = (f32[512,1]{1,0:T(8,128)}, f32[512,1]{1,0:T(8,128)S(1)}, u32[]{:S(2)}) copy-start(f32[512,1]{1,0:T(8,128)S(1)} %get-tuple-element.58.inverse_in) | copy-start | bytes 6148
  62.5 2.9 %copy-start.37 = (bf16[8,96,768]{2,1,0:T(8,128)(2,1)}, bf16[8,96,768]{2,1,0:T(8,128)(2,1)S(1)}, u32[]{:S(2)}) copy-start(bf16[8,96,768]{2,1,0:T(8,128)(2,1)S(1)} %get-tuple-element.50) | copy-start | bytes 3538948
  66.4 6.9 %copy-start.45 = (bf16[2,256,3,64]{1,0,3,2:T(2,128)(2,1)}, bf16[2,256,3,64]{1,0,3,2:T(2,128)(2,1)S(1)}, u32[]{:S(2)}) copy-start(bf16[2,256,3,64]{1,0,3,2:T(2,128)(2,1)S(1)} %convert_element_type.109) | copy-start | bytes 589828
  75.2 2.3 copy-start.30
  75.2 2.3 copy-start.35
  75.4 30.3 %copy-start.40 = (bf16[512,768]{1,0:T(8,128)(2,1)S(1)}, bf16[512,768]{1,0:T(8,128)(2,1)}, u32[]{:S(2)}) copy-start(bf16[512,768]{1,0:T(8,128)(2,1)} %copy-done.39) | copy-start | bytes 2359300
  105.7 0.9 copy-start.13
  105.7 1.1 copy-start.15
  105.7 1.2 copy-start.26
  105.7 3.9 %copy-start.42 = (bf16[512,768]{1,0:T(8,128)(2,1)}, bf16[512,768]{1,0:T(8,128)(2,1)S(1)}, u32[]{:S(2)}) copy-start(bf16[512,768]{1,0:T(8,128)(2,1)S(1)} %get-tuple-element.49) | copy-start | bytes 2359300
  105.8 2.1 copy-start.38
  105.8 2.1 copy-start.53
  109.6 2.0 copy-start.55
  109.6 2.0 copy-start.54
  113.4 3.5 %copy-start.41 = (bf16[512,768]{1,0:T(8,128)(2,1)S(1)}, bf16[512,768]{1,0:T(8,128)(2,1)}, u32[]{:S(2)}) copy-start(bf16[512,768]{1,0:T(8,128)(2,1)} %copy-done.39) | copy-start | bytes 2359300
  113.4 3.5 %copy-start.56 = (f32[512,768]{1,0:T(8,128)S(1)}, f32[512,768]{1,0:T(8,128)}, u32[]{:S(2)}) copy-start(f32[512,768]{1,0:T(8,128)} %copy-done.55) | copy-start | bytes 4718596
  116.9 1.1 copy-start.2
  116.9 1.4 copy-start.3
  116.9 1.5 copy-start.12
  116.9 1.7 copy-start.14
  117.0 1.8 copy-start.16
  117.0 1.9 copy-start.27
  117.0 1.8 copy-start.36
  150.9 2.8 %copy-start.18 = (f32[512,192]{1,0:T(8,128)S(1)}, f32[512,192]{1,0:T(8,128)}, u32[]{:S(2)}) copy-start(f32[512,192]{1,0:T(8,128)} %copy-done.17) | copy-start | bytes 1179652
  156.0 2.5 %copy-start.49 = (f32[2,256,3,64]{1,0,3,2:T(2,128)S(1)}, f32[2,256,3,64]{1,0,3,2:T(2,128)}, u32[]{:S(2)}) copy-start(f32[2,256,3,64]{1,0,3,2:T(2,128)} %squeeze.20) | copy-start | bytes 1179652
  156.0 2.5 %copy-start.50 = (bf16[2,256,3,64]{1,0,3,2:T(2,128)(2,1)S(1)}, bf16[2,256,3,64]{1,0,3,2:T(2,128)(2,1)}, u32[]{:S(2)}) copy-start(bf16[2,256,3,64]{1,0,3,2:T(2,128)(2,1)} %reshape.133) | copy-start | bytes 589828
  158.5 2.0 copy-start.44
  160.6 1.0 copy-start.43
  160.6 1.4 copy-start.46
  163.2 1.7 copy-start.5
  166.5 1.6 copy-start.1
  166.5 1.6 copy-start.34
  168.1 1.1 copy-start.6
  169.2 1.0 copy-start.8
  170.3 1.0 copy-start.10
  171.3 0.9 copy-start.25
  220.6 7.0 %copy-start.51 = (f32[16,1,256]{2,0,1:T(8,128)S(1)}, f32[16,1,256]{2,0,1:T(8,128)}, u32[]{:S(2)}) copy-start(f32[16,1,256]{2,0,1:T(8,128)} %copy.147) | copy-start | bytes 49156
  220.6 7.0 %copy-start.52 = (s32[16]{0:T(128)S(1)}, s32[16]{0:T(128)}, u32[]{:S(2)}) copy-start(s32[16]{0:T(128)} %fusion.45) | copy-start | bytes 196
  222.6 6.4 %copy-start.23 = (f32[3,96,192]{2,1,0:T(8,128)S(1)}, f32[3,96,192]{2,1,0:T(8,128)}, u32[]{:S(2)}) copy-start(f32[3,96,192]{2,1,0:T(8,128)} %copy-done.22) | copy-start | bytes 663556
  226.2 4.2 %copy-start.21 = (f32[96,768]{1,0:T(8,128)S(1)}, f32[96,768]{1,0:T(8,128)}, u32[]{:S(2)}) copy-start(f32[96,768]{1,0:T(8,128)} %copy-done.20) | copy-start | bytes 884740
  (9 other events, 6.8 us)
